TPU v7x, 256 devices: a whole 4x4x8 slice. The times are simulated.
256 devices in a mesh: fit: 4 (over x_lo, core), row: 64 (over y, x_hi, z).
Axes of the slice: x: 4 (x_hi: 2, x_lo: 2; x = x_hi * 2 + x_lo), y: 4, z: 8, core: 2. Of those that a mesh axis runs over, the one named last changes fastest.
Arguments:
- factors: bfloat16 [8192, 12, 512], P('row', 'fit'), may hold values from -2 to 2
Outputs:
- exchange: float32 [4, 8192, 2048], P('fit', 'row')
All inputs are finite; a program needn't handle non-finite values.
Results may differ from a plain program's by a relative error of at most 0.0003.
Values may be sent and summed in bfloat16 or wider, within the bound.
No kernel may reach another device: no remote copies, remote signals or barrier semaphores. Data moves between devices by JAX's collectives and lax.ppermute only.
A program may use at most 128 MiB of HBM per device.

v0:
```python
import jax
import jax.numpy as jnp
from jax import lax
from jax.sharding import PartitionSpec as P


def contribution(running, local_part, shard_rows, sub_width):
    groups = running.shape[0]
    product = lax.dot_general(
        local_part, shard_rows, (((1, 2), (1, 2)), ((), ())), preferred_element_type=jnp.float32
    )
    rows_here = product.shape[0]
    placed = jnp.transpose(product.reshape(rows_here, -1, groups, sub_width), (2, 0, 1, 3)).reshape(
        groups, rows_here, -1
    )
    return running + placed


def accumulate(local_rows, remote_rows, initial, sub_width):
    occupied = local_rows.shape[2]
    running = initial
    columns = occupied // 4
    for quarter in range(4):
        local_part = local_rows[:, :, quarter * columns : (quarter + 1) * columns]
        remote_part = remote_rows[:, :, quarter * columns : (quarter + 1) * columns]

        def add_quarter(state, shard_rows, first_row, local_part=local_part):
            return contribution(state, local_part, shard_rows, sub_width)

        running = add_quarter(
            running, lax.all_gather(remote_part, "row", axis=0, tiled=True), jnp.int32(0)
        )
    return running


def per_device(factors):
    row_count = factors.shape[0]
    blocks = lax.axis_size("row")
    groups = lax.axis_size("fit")
    sub_width = row_count // groups
    initial = jnp.zeros((groups, row_count, blocks * sub_width), jnp.float32)
    summed = accumulate(factors, factors, initial, sub_width)
    return lax.psum_scatter(summed, "fit", scatter_dimension=0, tiled=True)


def solution(mesh):
    return jax.shard_map(
        per_device,
        mesh=mesh,
        in_specs=(P("row", "fit", None),),
        out_specs=P("fit", "row", None),
        check_vma=False,
    )
```

profile of v0, /device:TPU:1, one launch (start us, length us, event | category | flops | bytes accessed | tf_op | source)
XLA Modules:
  0.0 648.0 jit_solution(8467610364659757598)
XLA Ops:
  6.5 0.0 all-gather.11.cloned.1.call-start
  6.5 1.8 fusion.7
  8.3 0.0 all-gather.11.cloned.1.call-update
  8.4 0.0 all-gather.9.cloned.1.call-start
  8.4 0.7 all-gather.9.cloned.1.call-update
  9.1 0.0 all-gather.7.cloned.1.call-start
  9.2 0.7 all-gather.7.cloned.1.call-update
  9.8 0.0 all-gather.5.cloned.1.call-start
  9.9 0.5 all-gather.5.cloned.1.call-update
  10.4 0.0 copy-start
  10.4 0.0 reduce-scatter.2.cloned.1.call-start
  10.5 140.7 %all-gather.11.cloned.1.call-done = bf16[8192,3,128]{2,0,1:T(8,128)(2,1)} async-done(((bf16[128,3,128]{2,0,1:T(8,128)(2,1)}), bf16[8192,3,128]{2,0,1:T(8,128)(2,1)}) %all-gather.11.cloned.1.call-update) | async-done | bytes 6291472 | tf_op jit(solution)/shard_map/all_gather | solution.py:31
  151.1 6.9 %convolution_bitcast_fusion = f32[128,8192]{1,0:T(8,128)} fusion(bf16[8192,3,128]{2,0,1:T(8,128)(2,1)} %all-gather.11.cloned.1.call-done, bf16[128,3,512]{2,0,1:T(8,128)(2,1)} %param.1), kind=kOutput, calls=%fused_computation | convolution fusion | flops 805306368 | bytes 10584064 | tf_op jit(solution)/shard_map/dot_general | solution.py:9
  158.0 132.8 %all-gather.9.cloned.1.call-done = bf16[8192,3,128]{2,0,1:T(8,128)(2,1)} async-done(((bf16[128,3,128]{2,0,1:T(8,128)(2,1)}), bf16[8192,3,128]{2,0,1:T(8,128)(2,1)}) %all-gather.9.cloned.1.call-update) | async-done | bytes 6291472 | tf_op jit(solution)/shard_map/all_gather | solution.py:31
  290.8 0.0 copy-done
  290.8 6.9 %convolution_bitcast_fusion.1 = f32[128,8192]{1,0:T(8,128)} fusion(bf16[8192,3,128]{2,0,1:T(8,128)(2,1)} %all-gather.9.cloned.1.call-done, bf16[128,3,512]{2,0,1:T(8,128)(2,1)S(1)} %copy-done), kind=kOutput, calls=%fused_computation.1 | convolution fusion | flops 805306368 | bytes 10584064 | tf_op jit(solution)/shard_map/dot_general | solution.py:9
  297.7 132.8 %all-gather.7.cloned.1.call-done = bf16[8192,3,128]{2,0,1:T(8,128)(2,1)} async-done(((bf16[128,3,128]{2,0,1:T(8,128)(2,1)}), bf16[8192,3,128]{2,0,1:T(8,128)(2,1)}) %all-gather.7.cloned.1.call-update) | async-done | bytes 6291472 | tf_op jit(solution)/shard_map/all_gather | solution.py:31
  430.5 6.8 %convolution_bitcast_fusion.2 = f32[128,8192]{1,0:T(8,128)} fusion(bf16[8192,3,128]{2,0,1:T(8,128)(2,1)} %all-gather.7.cloned.1.call-done, bf16[128,3,512]{2,0,1:T(8,128)(2,1)S(1)} %copy-done), kind=kOutput, calls=%fused_computation.2 | convolution fusion | flops 805306368 | bytes 10584064 | tf_op jit(solution)/shard_map/dot_general | solution.py:9
  437.3 132.8 %all-gather.5.cloned.1.call-done = bf16[8192,3,128]{2,0,1:T(8,128)(2,1)} async-done(((bf16[128,3,128]{2,0,1:T(8,128)(2,1)}), bf16[8192,3,128]{2,0,1:T(8,128)(2,1)}) %all-gather.5.cloned.1.call-update) | async-done | bytes 6291472 | tf_op jit(solution)/shard_map/all_gather | solution.py:31
  570.1 10.5 %fusion.2 = f32[128,8192]{1,0:T(8,128)} fusion(f32[128,8192]{1,0:T(8,128)} %convolution_bitcast_fusion, f32[128,8192]{1,0:T(8,128)} %convolution_bitcast_fusion.1, f32[128,8192]{1,0:T(8,128)} %convolution_bitcast_fusion.2, bf16[8192,3,128]{2,0,1:T(8,128)(2,1)} %all-gather.5.cloned.1.call-done, bf16[128,3,512]{2,0,1:T(8,128)(2,1)S(1)} %copy-done), kind=kOutput, calls=%fused_computation.6 | convolution fusion | flops 808452096 | bytes 23166976 | tf_op jit(solution)/shard_map/dot_general | solution.py:9
  580.6 5.6 copy.3
  586.2 4.8 copy.4
  590.9 0.0 reduce-scatter.2.cloned.1.call-update
  590.9 48.0 %reduce-scatter.2.cloned.1.call-done = f32[1,128,2048]{1,2,0:T(8,128)} async-done(((f32[4,128,2048]{1,2,0:T(8,128)}), f32[1,128,2048]{1,2,0:T(8,128)}) %reduce-scatter.2.cloned.1.call-update) | async-done | bytes 1048592 | tf_op jit(solution)/shard_map/reduce_scatter | solution.py:43
  639.0 2.5 copy.5
Async XLA Ops:
  6.5 144.6 %all-gather.11.cloned.1.call-start = ((), (), s32[]{:S(2)}) async-start(), calls=%async_computation.4 | async-start | bytes 6389760 | tf_op jit(solution)/shard_map/all_gather | solution.py:31
  8.4 282.5 %all-gather.9.cloned.1.call-start = ((), (), s32[]{:S(2)}) async-start(), calls=%async_computation.3 | async-start | bytes 6389760 | tf_op jit(solution)/shard_map/all_gather | solution.py:31
  9.1 421.4 %all-gather.7.cloned.1.call-start = ((), (), s32[]{:S(2)}) async-start(), calls=%async_computation.2 | async-start | bytes 6389760 | tf_op jit(solution)/shard_map/all_gather | solution.py:31
  9.8 560.2 %all-gather.5.cloned.1.call-start = ((), (), s32[]{:S(2)}) async-start(), calls=%async_computation.1 | async-start | bytes 6389760 | tf_op jit(solution)/shard_map/all_gather | solution.py:31
  10.4 280.4 %copy-start = (bf16[128,3,512]{2,0,1:T(8,128)(2,1)S(1)}, bf16[128,3,512]{2,0,1:T(8,128)(2,1)}, u32[]{:S(2)}) copy-start(bf16[128,3,512]{2,0,1:T(8,128)(2,1)} %param.1) | copy-start | bytes 1179652
  10.4 628.5 %reduce-scatter.2.cloned.1.call-start = ((), (), s32[]{:S(2)}) async-start(), calls=%async_computation.5 | async-start | bytes 5242880 | tf_op jit(solution)/shard_map/reduce_scatter | solution.py:43
Sparse Core Ops, SparseCore 0:
  10.9 140.2 all-gather.10
  154.7 136.1 all-gather.8
  294.4 136.1 all-gather.6
  433.9 136.1 all-gather.4
  591.1 47.8 reduce-scatter.1
where the time goes:
time: 648 us
  waiting for transfers between devices  589 us (91%)
  matrix products  31 us (5%)
  local copies, waits for them, and re-layouts  14.7 us (2%)
  between operations  13.2 us (2%)
    all_gather x4, waiting for transfers between devices, accumulate(): lax.all_gather(remote_part, 'row', axis=0, tiled=True)  539 us
    reduce_scatter x1, waiting for transfers between devices, per_device(): return lax.psum_scatter(summed, 'fit', scatter_dimension=0, tiled=True)  48 us
    dot_general x4, matrix products, contribution(): lax.dot_general(local_part, shard_rows, (((1, 2), (1, 2)), ((), ())), pre...  31 us
  transfers between devices with their start and end apart: 5, of which 5 were waited for; matrix products, arithmetic and copies ran while one was open for 3% of the time, Pallas kernels for 0%

commit v1 on v0

v1 whole, which is shorter than its diff:
```python
import jax
import jax.numpy as jnp
from jax import lax
from jax.sharding import Mesh, PartitionSpec as P


def split_mesh(mesh):
    groups, rows = mesh.devices.shape
    cores, highs, lines = 2, 2, 8
    return Mesh(
        mesh.devices.reshape(groups // cores, cores, rows // (highs * lines), highs, lines),
        ("xl", "core", "y", "xh", "z"),
    )


def per_device(factors):
    rows, aux, occ = factors.shape
    local = factors.reshape(rows, aux * occ)
    groups = 4
    sub = rows // groups
    left = lax.all_gather(local, ("y", "xh"), axis=0, tiled=True)
    right = lax.all_gather(local, "z", axis=0, tiled=True)
    lines = lax.axis_size("z")
    planes = lax.axis_size(("y", "xh"))
    right = right.reshape(lines, groups, sub, aux * occ).transpose(1, 0, 2, 3).reshape(groups, lines * sub, aux * occ)
    product = lax.dot_general(
        right, left, (((2,), (1,)), ((), ())), preferred_element_type=jnp.float32
    )
    product = product.transpose(0, 2, 1)
    mine = lax.psum_scatter(product, ("xl", "core"), scatter_dimension=0, tiled=True)
    mine = mine.reshape(planes, rows, lines * sub)
    swapped = lax.all_to_all(mine, ("y", "xh"), split_axis=0, concat_axis=0, tiled=True)
    out = swapped.transpose(1, 0, 2).reshape(1, rows, planes * lines * sub)
    return out


def solution(mesh):
    return jax.shard_map(
        per_device,
        mesh=split_mesh(mesh),
        in_specs=(P(("y", "xh", "z"), ("xl", "core"), None),),
        out_specs=P(("xl", "core"), ("y", "xh", "z"), None),
        check_vma=False,
    )
```

time: 648 us -> 223 us (0.34)
  waiting for transfers between devices: 589 us -> 167 us
  matrix products: 31 us -> 8.23 us
  blocking collectives: 0 us -> 22.2 us
    all_gather x4 -> x2, waiting for transfers between devices: 539 us -> 120 us  [the longest x1 66.4 us: per_device(): left = lax.all_gather(local, ('y', 'xh'), axis=0, tiled=True)]
    dot_general x4 -> x1, matrix products: 31 us -> 8.23 us  [per_device(): lax.dot_general(right, left, (((2,), (1,)), ((), ())), preferred_element_...]
    all_to_all x0 -> x1, blocking collectives: none -> 22.2 us  [per_device(): lax.all_to_all(mine, ('y', 'xh'), split_axis=0, concat_axis=0, tiled=True)]
    add x2 -> x0, local copies, waits for them, and re-layouts: 10.3 us -> none  [contribution(): return running + placed]
  transfers between devices with their start and end apart: 5 -> 3, of which waited for: 5 -> 3; matrix products, arithmetic and copies ran while one was open for 3% -> 3% of each run, Pallas kernels for 0% -> 0%
where the time goes in v1:
time: 223 us
  waiting for transfers between devices  167 us (75%)
  blocking collectives  22.2 us (10%)
  between operations  13.1 us (6%)
  local copies, waits for them, and re-layouts  11.9 us (5%)
  matrix products  8.23 us (4%)
    all_gather x1, waiting for transfers between devices, per_device(): left = lax.all_gather(local, ('y', 'xh'), axis=0, tiled=True)  66.4 us
    all_gather x1, waiting for transfers between devices, per_device(): right = lax.all_gather(local, 'z', axis=0, tiled=True)  54 us
    reduce_scatter x1, waiting for transfers between devices, per_device(): lax.psum_scatter(product, ('xl', 'core'), scatter_dimension=0, tiled=True)  46.7 us
    all_to_all x1, blocking collectives, per_device(): lax.all_to_all(mine, ('y', 'xh'), split_axis=0, concat_axis=0, tiled=True)  22.2 us
    dot_general x1, matrix products, per_device(): lax.dot_general(right, left, (((2,), (1,)), ((), ())), preferred_element_...  8.23 us
  transfers between devices with their start and end apart: 3, of which 3 were waited for; matrix products, arithmetic and copies ran while one was open for 3% of the time, Pallas kernels for 0%

profile of v1, /device:TPU:1, one launch (start us, length us, event | category | flops | bytes accessed | tf_op | source)
XLA Modules:
  0.0 222.6 jit_solution(17575365184044722533)
XLA Ops:
  6.5 0.0 all-gather.3.cloned.1.call-start
  6.5 1.9 copy.14
  8.5 0.0 all-gather.3.cloned.1.call-update
  8.5 0.0 all-gather.5.cloned.1.call-start
  8.5 1.9 copy.17
  10.4 0.0 all-gather.5.cloned.1.call-update
  10.5 0.0 reduce-scatter.2.cloned.1.call-start
  10.5 54.0 %all-gather.3.cloned.1.call-done = bf16[1024,1536]{0,1:T(8,128)(2,1)} async-done(((bf16[128,1536]{0,1:T(8,128)(2,1)}), bf16[1024,1536]{0,1:T(8,128)(2,1)}) %all-gather.3.cloned.1.call-update) | async-done | bytes 3145744 | tf_op jit(solution)/shard_map/all_gather | solution.py:22
  64.5 3.2 %copy.15 = bf16[1024,1536]{1,0:T(8,128)(2,1)S(1)} copy(bf16[1024,1536]{0,1:T(8,128)(2,1)} %all-gather.3.cloned.1.call-done) | data formatting | bytes 6291456 | tf_op jit(solution)/shard_map/all_gather | solution.py:22
  67.7 1.9 copy.16
  69.6 66.4 %all-gather.5.cloned.1.call-done = bf16[1024,1536]{1,0:T(8,128)(2,1)} async-done(((bf16[128,1536]{1,0:T(8,128)(2,1)}), bf16[1024,1536]{1,0:T(8,128)(2,1)}) %all-gather.5.cloned.1.call-update) | async-done | bytes 3145744 | tf_op jit(solution)/shard_map/all_gather | solution.py:21
  136.0 8.2 %fusion.2 = f32[4,1024,256]{1,2,0:T(8,128)} fusion(bf16[4,256,1536]{2,1,0:T(8,128)(2,1)} %bitcast.26, bf16[1024,1536]{1,0:T(8,128)(2,1)} %all-gather.5.cloned.1.call-done), kind=kOutput, calls=%fused_computation.2 | convolution fusion | flops 3221225472 | bytes 10485760 | tf_op jit(solution)/shard_map/dot_general | solution.py:26
  144.2 0.0 reduce-scatter.2.cloned.1.call-update
  144.3 46.7 %reduce-scatter.2.cloned.1.call-done = f32[1,1024,256]{1,2,0:T(8,128)} async-done(((f32[4,1024,256]{1,2,0:T(8,128)}), f32[1,1024,256]{1,2,0:T(8,128)}) %reduce-scatter.2.cloned.1.call-update) | async-done | bytes 1048592 | tf_op jit(solution)/shard_map/reduce_scatter | solution.py:30
  190.9 1.4 copy.20
  192.3 0.2 copy.18
  192.6 22.2 %all_to_all.5 = f32[8,128,256]{1,2,0:T(8,128)S(1)} all-to-all(f32[8,128,256]{1,2,0:T(8,128)S(1)} %copy.18), channel_id=1, replica_groups=mesh['xl'=2,'core'=2,'y'=4,'xh'=2,'z'=8] {'y','xh'}, dimensions={0} | all-to-all | bytes 2097152 | tf_op jit(solution)/shard_map/all_to_all | solution.py:32
  214.8 1.3 copy.19
Async XLA Ops:
  6.5 58.0 %all-gather.3.cloned.1.call-start = ((), (), s32[]{:S(2)}) async-start(), calls=%async_computation.2 | async-start | bytes 3538944 | tf_op jit(solution)/shard_map/all_gather | solution.py:22
  8.5 127.5 %all-gather.5.cloned.1.call-start = ((), (), s32[]{:S(2)}) async-start(), calls=%async_computation.3 | async-start | bytes 3538944 | tf_op jit(solution)/shard_map/all_gather | solution.py:21
  10.5 180.5 %reduce-scatter.2.cloned.1.call-start = ((), (), s32[]{:S(2)}) async-start(), calls=%async_computation.4 | async-start | bytes 5242880 | tf_op jit(solution)/shard_map/reduce_scatter | solution.py:30
Sparse Core Ops, SparseCore 0:
  9.1 55.3 all-gather.2
  67.1 68.8 all-gather.4
  144.4 46.4 reduce-scatter.1

commit v2 on v1

v2 whole, which is shorter than its diff:
```python
import functools

import jax
import jax.numpy as jnp
from jax import lax
from jax.experimental import pallas as pl
from jax.experimental.pallas import tpu as pltpu
from jax.sharding import Mesh, PartitionSpec as P

XL, CORE, Y, XH, Z = 2, 2, 4, 2, 8
AXES = ("xl", "core", "y", "xh", "z")


def split_mesh(mesh):
    return Mesh(mesh.devices.reshape(XL, CORE, Y, XH, Z), AXES)


def move(value, axes, target):
    sizes = {"xl": XL, "core": CORE, "y": Y, "xh": XH, "z": Z}
    dims = [sizes[a] for a in axes]
    count = 1
    for d in dims:
        count *= d
    pairs = []
    for source in range(count):
        rest, place = source, []
        for d in reversed(dims):
            place.insert(0, rest % d)
            rest //= d
        goal = target(*place)
        flat = 0
        for d, g in zip(dims, goal):
            flat = flat * d + g % d
        pairs.append((source, flat))
    return lax.ppermute(value, axes, pairs)


def turn(core, step):
    return step if core == 0 else -step


def along_z(value, step):
    return move(value, ("core", "z"), lambda c, z: (c, z + turn(c, step)))


def along_y(value, step):
    return move(value, ("core", "y"), lambda c, y: (c, y + turn(c, step)))


def across(value):
    return move(value, ("xh",), lambda h: (h + 1,))


def product_kernel(order, *refs):
    row_blocks, column_blocks = refs[:8], refs[8:16]
    send, keep, rows, columns, sems = refs[16:]
    aux, height, occ = row_blocks[0].shape
    copies = []
    for k in range(8):
        for a in range(aux):
            copies.append(
                pltpu.make_async_copy(
                    column_blocks[k].at[a],
                    columns.at[order[8 + k], :, pl.ds(a * occ, occ)],
                    sems.at[k * aux + a],
                )
            )
            copies.append(
                pltpu.make_async_copy(
                    row_blocks[k].at[a],
                    rows.at[order[k], :, pl.ds(a * occ, occ)],
                    sems.at[(8 + k) * aux + a],
                )
            )
    for c in copies:
        c.start()
    for c in copies:
        c.wait()
    sub = height // 4
    for slot in range(4):
        target = send if slot < 2 else keep
        first = pl.multiple_of(order[16 + slot] * sub, sub)
        picked = columns[:, pl.ds(first, sub), :].reshape(8 * sub, aux * occ)

        @pl.loop(0, 8)
        def _(k):
            target[slot % 2, k] = lax.dot_general(
                rows[k], picked, (((1,), (1,)), ((), ())), preferred_element_type=jnp.float32
            )


def products(order, row_blocks, column_blocks):
    aux, height, occ = row_blocks[0].shape
    shape = jax.ShapeDtypeStruct((2, 8, height, 2 * height), jnp.float32)
    return pl.pallas_call(
        product_kernel,
        out_shape=[shape, shape],
        in_specs=[pl.BlockSpec(memory_space=pltpu.SMEM)] + [pl.BlockSpec(memory_space=pl.ANY)] * 16,
        out_specs=[pl.BlockSpec(memory_space=pltpu.VMEM)] * 2,
        scratch_shapes=[
            pltpu.VMEM((8, height, aux * occ), jnp.bfloat16),
            pltpu.VMEM((8, height, aux * occ), jnp.bfloat16),
            pltpu.SemaphoreType.DMA((16 * aux,)),
        ],
        compiler_params=pltpu.CompilerParams(vmem_limit_bytes=32 * 1024 * 1024),
    )(order, *row_blocks, *column_blocks)


def assemble_kernel(order, *refs):
    out = refs[-1]
    for k in range(4):
        for h in range(2):
            first = pl.multiple_of(order[2 * k + h] * 256, 256)
            out[0, :, pl.ds(first, 256)] = refs[k][h]


def assemble(order, pieces):
    height = pieces[0].shape[1]
    return pl.pallas_call(
        assemble_kernel,
        out_shape=jax.ShapeDtypeStruct((1, height, 2048), jnp.float32),
        in_specs=[pl.BlockSpec(memory_space=pltpu.SMEM)] + [pl.BlockSpec(memory_space=pltpu.VMEM)] * 4,
        out_specs=pl.BlockSpec(memory_space=pltpu.VMEM),
    )(order, *pieces)


def per_device(factors):
    own = jnp.transpose(factors, (1, 0, 2))
    xl, core, y, xh, z = (lax.axis_index(a) for a in AXES)
    sign = 1 - 2 * core

    za1 = along_z(own, 1)
    zb1 = along_z(own, -1)
    ya1 = along_y(own, 1)
    yb1 = along_y(own, -1)
    x0 = across(own)
    za2 = along_z(za1, 1)
    zb2 = along_z(zb1, -1)
    ya2 = along_y(ya1, 1)
    xa1 = along_y(x0, 1)
    xb1 = along_y(x0, -1)
    za3 = along_z(za2, 1)
    zb3 = along_z(zb2, -1)
    xa2 = across(ya2)
    za4 = along_z(za3, 1)

    row_blocks = [own, ya1, yb1, ya2, x0, xa1, xb1, xa2]
    dy = [0, -sign, sign, 2]
    row_order = [dx * 4 + lax.rem(d + 4, 4) for dx in range(2) for d in dy]
    column_blocks = [own, za1, zb1, za2, zb2, za3, zb3, za4]
    dz = [0, -sign, sign, -2 * sign, 2 * sign, -3 * sign, 3 * sign, 4]
    column_order = [lax.rem(z + d + 8, 8) for d in dz]
    fit_order = [
        (1 - xl) * 2 + 1 - core,
        xl * 2 + 1 - core,
        (1 - xl) * 2 + core,
        xl * 2 + core,
    ]
    order = jnp.stack([jnp.int32(v) for v in row_order + column_order + fit_order])
    send, keep = products(order, row_blocks, column_blocks)
    summed = keep + move(send, ("core",), lambda c: (c + 1,))
    summed = summed.reshape(2, 2, 4, *summed.shape[2:])

    near = move(summed[0, 0], ("xl",), lambda a: (a + 1,))
    cross = move(summed[0, 1], ("xl", "xh"), lambda a, h: (a + 1, h + 1))
    far = across(summed[1, 1])
    t = jnp.stack([summed[1, 0] + near, cross + far], axis=1)
    pieces = [t[0]] + [move(t[d], ("y",), lambda b, d=d: (b + d,)) for d in range(1, 4)]
    places = [lax.rem(y - d + 4, 4) * 2 + lax.rem(xh + h, 2) for d in range(4) for h in range(2)]
    return assemble(jnp.stack(places).astype(jnp.int32), pieces)


def solution(mesh):
    return jax.shard_map(
        per_device,
        mesh=split_mesh(mesh),
        in_specs=(P(("y", "xh", "z"), ("xl", "core"), None),),
        out_specs=P(("xl", "core"), ("y", "xh", "z"), None),
        check_vma=False,
    )
```

time: 223 us -> 117 us (0.52)
  waiting for transfers between devices: 167 us -> 54.5 us
  starting transfers between devices: 0.09 us -> 39.8 us
  blocking collectives: 22.2 us -> 0 us
  Pallas kernels: 0 us -> 17.8 us
  between operations: 13.1 us -> 0.07 us
  local copies, waits for them, and re-layouts: 11.9 us -> 2.63 us
  matrix products: 8.23 us -> 0 us
    all_gather x2 -> x0, waiting for transfers between devices: 120 us -> none  [the longest x1 66.4 us: per_device(): left = lax.all_gather(local, ('y', 'xh'), axis=0, tiled=True)]
    ppermute x0 -> x21, waiting for transfers between devices: none -> 54.5 us  [move(): return lax.ppermute(value, axes, pairs)]
    reduce_scatter x1 -> x0, waiting for transfers between devices: 46.7 us -> none  [per_device(): lax.psum_scatter(product, ('xl', 'core'), scatter_dimension=0, tiled=True)]
    ppermute x0 -> x21, starting transfers between devices: none -> 39.8 us  [move(): return lax.ppermute(value, axes, pairs)]
    all_to_all x1 -> x0, blocking collectives: 22.2 us -> none  [per_device(): lax.all_to_all(mine, ('y', 'xh'), split_axis=0, concat_axis=0, tiled=True)]
    pallas_call x0 -> x2, Pallas kernels: none -> 17.8 us  [the longest x1 15.6 us: products(): pl.pallas_call(product_kernel, out_shape=[shape, shape], in_specs=[pl.Blo...]
    dot_general x1 -> x0, matrix products: 8.23 us -> none  [per_device(): lax.dot_general(right, left, (((2,), (1,)), ((), ())), preferred_element_...]
    reshape x3 -> x0, local copies, waits for them, and re-layouts: 3.42 us -> none  [the longest x1 1.91 us: per_device(): local = factors.reshape(rows, aux * occ)]
  transfers between devices with their start and end apart: 3 -> 21, of which waited for: 3 -> 11; matrix products, arithmetic and copies ran while one was open for 3% -> 1% of each run, Pallas kernels for 0% -> 0%
where the time goes in v2:
time: 117 us; the launch traced here: 116 us
  waiting for transfers between devices  54.5 us (47%)
  starting transfers between devices  39.8 us (34%)
  Pallas kernels  17.8 us (15%)
  local copies, waits for them, and re-layouts  2.63 us (2%)
  other arithmetic  1.19 us (1%)
    ppermute x21, waiting for transfers between devices, move(): return lax.ppermute(value, axes, pairs)  54.5 us
    ppermute x21, starting transfers between devices, move(): return lax.ppermute(value, axes, pairs)  39.8 us
    pallas_call x1, Pallas kernels, products(): pl.pallas_call(product_kernel, out_shape=[shape, shape], in_specs=[pl.Blo...  15.6 us
  transfers between devices with their start and end apart: 21, of which 11 were waited for; matrix products, arithmetic and copies ran while one was open for 1% of the time, Pallas kernels for 0%

profile of v2, /device:TPU:1, one launch (start us, length us, event | category | flops | bytes accessed | tf_op | source)
XLA Modules:
  0.0 116.0 jit_solution(8440478119230786012)
XLA Ops:
  0.0 6.4 %collective-permute-start.7 = (bf16[3,128,512]{2,1,0:T(8,128)(2,1)}, bf16[3,128,512]{2,1,0:T(8,128)(2,1)S(1)}, u32[]{:S(2)}, u32[]{:S(2)}) collective-permute-start(bf16[3,128,512]{2,1,0:T(8,128)(2,1)} %bitcast.52), channel_id=1, source_target_pairs={{0,1},{1,2},{2,3},{3,4},{4,5},{5,6},{6,7},{7,0},{64,71},{65,64},{6... | collective-permute-start | bytes 1179656 | tf_op jit(solution)/shard_map/ppermute | solution.py:35
  6.4 0.0 collective-permute-start.8
  6.4 2.7 %collective-permute-start = (bf16[3,128,512]{2,1,0:T(8,128)(2,1)}, bf16[3,128,512]{2,1,0:T(8,128)(2,1)S(1)}, u32[]{:S(2)}, u32[]{:S(2)}) collective-permute-start(bf16[3,128,512]{2,1,0:T(8,128)(2,1)} %bitcast.54), channel_id=1, source_target_pairs={{0,16},{16,32},{32,48},{48,0},{64,112},{80,64},{96,80},{112,96},{1... | collective-permute-start | bytes 1179656 | tf_op jit(solution)/shard_map/ppermute | solution.py:35
  9.1 5.4 %collective-permute-done.7.refs_9_ = bf16[3,128,512]{2,1,0:T(8,128)(2,1)S(1)} collective-permute-done((bf16[3,128,512]{2,1,0:T(8,128)(2,1)}, bf16[3,128,512]{2,1,0:T(8,128)(2,1)S(1)}, u32[]{:S(2)}, u32[]{:S(2)}) %collective-permute-start.7) | collective-permute-done | bytes 393248 | tf_op jit(solution)/shard_map/ppermute | solution.py:35
  14.5 3.3 %collective-permute-start.9 = (bf16[3,128,512]{2,1,0:T(8,128)(2,1)S(1)}, bf16[3,128,512]{2,1,0:T(8,128)(2,1)S(1)}, u32[]{:S(2)}, u32[]{:S(2)}) collective-permute-start(bf16[3,128,512]{2,1,0:T(8,128)(2,1)S(1)} %collective-permute-done.7.refs_9_), channel_id=1, source_target_pairs={{0,1},{1,2},{2,3},{3,4},{4,5},{5,6},{6,7},{7,0},{64,71},{65,64},{6... | collective-permute-start | bytes 1179656 | tf_op jit(solution)/shard_map/ppermute | solution.py:35
  17.8 2.7 %collective-permute-start.3 = (bf16[3,128,512]{2,1,0:T(8,128)(2,1)}, bf16[3,128,512]{2,1,0:T(8,128)(2,1)S(1)}, u32[]{:S(2)}, u32[]{:S(2)}) collective-permute-start(bf16[3,128,512]{2,1,0:T(8,128)(2,1)} %bitcast.55), channel_id=1, source_target_pairs={{0,8},{8,0},{1,9},{9,1},{2,10},{10,2},{3,11},{11,3},{4,12},{12,4},... | collective-permute-start | bytes 1179656 | tf_op jit(solution)/shard_map/ppermute | solution.py:35
  20.6 1.3 %collective-permute-start.1 = (bf16[3,128,512]{2,1,0:T(8,128)(2,1)}, bf16[3,128,512]{2,1,0:T(8,128)(2,1)S(1)}, u32[]{:S(2)}, u32[]{:S(2)}) collective-permute-start(bf16[3,128,512]{2,1,0:T(8,128)(2,1)} %bitcast.56), channel_id=1, source_target_pairs={{0,48},{16,0},{32,16},{48,32},{64,80},{80,96},{96,112},{112,64},{1... | collective-permute-start | bytes 1179656 | tf_op jit(solution)/shard_map/ppermute | solution.py:35
  21.8 0.0 collective-permute-done.8.refs_10_
  21.9 0.0 collective-permute-start.10
  21.9 0.0 collective-permute-done.refs_1_
  21.9 1.5 %collective-permute-start.2 = (bf16[3,128,512]{2,1,0:T(8,128)(2,1)S(1)}, bf16[3,128,512]{2,1,0:T(8,128)(2,1)S(1)}, u32[]{:S(2)}, u32[]{:S(2)}) collective-permute-start(bf16[3,128,512]{2,1,0:T(8,128)(2,1)S(1)} %collective-permute-done.refs_1_), channel_id=1, source_target_pairs={{0,16},{16,32},{32,48},{48,0},{64,112},{80,64},{96,80},{112,96},{1... | collective-permute-start | bytes 1179656 | tf_op jit(solution)/shard_map/ppermute | solution.py:35
  23.4 2.6 %collective-permute-start.11 = (bf16[3,128,512]{2,1,0:T(8,128)(2,1)S(1)}, bf16[3,128,512]{2,1,0:T(8,128)(2,1)S(1)}, u32[]{:S(2)}, u32[]{:S(2)}) collective-permute-start(bf16[3,128,512]{2,1,0:T(8,128)(2,1)S(1)} %collective-permute-done.9.refs_11_), channel_id=1, source_target_pairs={{0,1},{1,2},{2,3},{3,4},{4,5},{5,6},{6,7},{7,0},{64,71},{65,64},{6... | collective-permute-start | bytes 1179656 | tf_op jit(solution)/shard_map/ppermute | solution.py:35
  26.0 2.7 %collective-permute-done.3.refs_4_ = bf16[3,128,512]{2,1,0:T(8,128)(2,1)S(1)} collective-permute-done((bf16[3,128,512]{2,1,0:T(8,128)(2,1)}, bf16[3,128,512]{2,1,0:T(8,128)(2,1)S(1)}, u32[]{:S(2)}, u32[]{:S(2)}) %collective-permute-start.3) | collective-permute-done | bytes 393248 | tf_op jit(solution)/shard_map/ppermute | solution.py:35
  28.7 1.3 %collective-permute-start.5 = (bf16[3,128,512]{2,1,0:T(8,128)(2,1)S(1)}, bf16[3,128,512]{2,1,0:T(8,128)(2,1)}, u32[]{:S(2)}, u32[]{:S(2)}) collective-permute-start(bf16[3,128,512]{2,1,0:T(8,128)(2,1)S(1)} %collective-permute-done.3.refs_4_), channel_id=1, source_target_pairs={{0,48},{16,0},{32,16},{48,32},{64,80},{80,96},{96,112},{112,64},{1... | collective-permute-start | bytes 1179656 | tf_op jit(solution)/shard_map/ppermute | solution.py:35
  30.0 2.0 %collective-permute-start.4 = (bf16[3,128,512]{2,1,0:T(8,128)(2,1)S(1)}, bf16[3,128,512]{2,1,0:T(8,128)(2,1)}, u32[]{:S(2)}, u32[]{:S(2)}) collective-permute-start(bf16[3,128,512]{2,1,0:T(8,128)(2,1)S(1)} %collective-permute-done.3.refs_4_), channel_id=1, source_target_pairs={{0,16},{16,32},{32,48},{48,0},{64,112},{80,64},{96,80},{112,96},{1... | collective-permute-start | bytes 1179656 | tf_op jit(solution)/shard_map/ppermute | solution.py:35
  31.9 0.0 collective-permute-done.2.refs_3_
  31.9 2.6 %collective-permute-start.6 = (bf16[3,128,512]{2,1,0:T(8,128)(2,1)S(1)}, bf16[3,128,512]{2,1,0:T(8,128)(2,1)}, u32[]{:S(2)}, u32[]{:S(2)}) collective-permute-start(bf16[3,128,512]{2,1,0:T(8,128)(2,1)S(1)} %collective-permute-done.2.refs_3_), channel_id=1, source_target_pairs={{0,8},{8,0},{1,9},{9,1},{2,10},{10,2},{3,11},{11,3},{4,12},{12,4},... | collective-permute-start | bytes 1179656 | tf_op jit(solution)/shard_map/ppermute | solution.py:35
  34.5 3.2 %collective-permute-start.13 = (bf16[3,128,512]{2,1,0:T(8,128)(2,1)S(1)}, bf16[3,128,512]{2,1,0:T(8,128)(2,1)}, u32[]{:S(2)}, u32[]{:S(2)}) collective-permute-start(bf16[3,128,512]{2,1,0:T(8,128)(2,1)S(1)} %collective-permute-done.11.refs_13_), channel_id=1, source_target_pairs={{0,1},{1,2},{2,3},{3,4},{4,5},{5,6},{6,7},{7,0},{64,71},{65,64},{6... | collective-permute-start | bytes 1179656 | tf_op jit(solution)/shard_map/ppermute | solution.py:35
  37.7 0.1 stack.112.order
  37.8 3.2 %collective-permute-done.5.refs_6_ = bf16[3,128,512]{2,1,0:T(8,128)(2,1)} collective-permute-done((bf16[3,128,512]{2,1,0:T(8,128)(2,1)S(1)}, bf16[3,128,512]{2,1,0:T(8,128)(2,1)}, u32[]{:S(2)}, u32[]{:S(2)}) %collective-permute-start.5) | collective-permute-done | bytes 393248 | tf_op jit(solution)/shard_map/ppermute | solution.py:35
  41.1 0.0 collective-permute-done.4.refs_5_
  41.1 0.0 collective-permute-done.12.refs_14_
  41.1 0.0 collective-permute-done.6.refs_7_
  41.1 5.3 %collective-permute-done.13.refs_15_ = bf16[3,128,512]{2,1,0:T(8,128)(2,1)} collective-permute-done((bf16[3,128,512]{2,1,0:T(8,128)(2,1)S(1)}, bf16[3,128,512]{2,1,0:T(8,128)(2,1)}, u32[]{:S(2)}, u32[]{:S(2)}) %collective-permute-start.13) | collective-permute-done | bytes 393248 | tf_op jit(solution)/shard_map/ppermute | solution.py:35
  46.3 1.0 copy-done
  47.3 15.6 %shard_map.17 = (f32[2,8,128,256]{3,2,1,0:T(8,128)S(1)}, f32[2,8,128,256]{3,2,1,0:T(8,128)S(1)}) custom-call(s32[20]{0:T(128)S(1)} %stack.112.order, bf16[3,128,512]{2,1,0:T(8,128)(2,1)S(1)} %bitcast.57, bf16[3,128,512]{2,1,0:T(8,128)(2,1)S(1)} %collective-permute-done.refs_1_, bf16[3,128,512]{2,1,0:T(8,128)(2,1)S(1)} %collective-permute-done.1.refs_2_, ...), custom_call_target="tpu_custom_call" | custom-call | tf_op jit(solution)/shard_map/pallas_call | solution.py:95
  62.9 1.2 %collective-permute-start.14 = (f32[2,8,128,256]{3,2,1,0:T(8,128)S(1)}, f32[2,8,128,256]{3,2,1,0:T(8,128)S(1)}, u32[]{:S(2)}, u32[]{:S(2)}) collective-permute-start(f32[2,8,128,256]{3,2,1,0:T(8,128)S(1)} %get-tuple-element.8), channel_id=1, source_target_pairs={{0,64},{64,0},{1,65},{65,1},{2,66},{66,2},{3,67},{67,3},{4,68},{68... | collective-permute-start | bytes 6291464 | tf_op jit(solution)/shard_map/ppermute | solution.py:35
  64.1 3.8 %collective-permute-done.14 = f32[2,8,128,256]{3,2,1,0:T(8,128)S(1)} collective-permute-done((f32[2,8,128,256]{3,2,1,0:T(8,128)S(1)}, f32[2,8,128,256]{3,2,1,0:T(8,128)S(1)}, u32[]{:S(2)}, u32[]{:S(2)}) %collective-permute-start.14) | collective-permute-done | bytes 2097184 | tf_op jit(solution)/shard_map/ppermute | solution.py:35
  67.9 0.3 add.171
  68.2 0.2 slice_bitcast_fusion
  68.3 0.3 collective-permute-start.15
  68.6 3.9 %collective-permute-start.17 = (f32[4,128,256]{2,1,0:T(8,128)S(1)}, f32[4,128,256]{2,1,0:T(8,128)S(1)}, u32[]{:S(2)}, u32[]{:S(2)}) collective-permute-start(f32[4,128,256]{2,1,0:T(8,128)S(1)} %get-tuple-element.9), channel_id=1, source_target_pairs={{0,8},{8,0},{1,9},{9,1},{2,10},{10,2},{3,11},{11,3},{4,12},{12,4},... | collective-permute-start | bytes 1572872 | tf_op jit(solution)/shard_map/ppermute | solution.py:35
  72.6 0.2 collective-permute-start.16
  72.8 8.8 %collective-permute-done.15 = f32[4,128,256]{2,1,0:T(8,128)S(1)} collective-permute-done((f32[4,128,256]{2,1,0:T(8,128)S(1)}, f32[4,128,256]{2,1,0:T(8,128)S(1)}, u32[]{:S(2)}, u32[]{:S(2)}) %collective-permute-start.15) | collective-permute-done | bytes 524320 | tf_op jit(solution)/shard_map/ppermute | solution.py:35
  81.6 0.1 fusion.1
  81.6 14.1 %collective-permute-done.17 = f32[4,128,256]{2,1,0:T(8,128)S(1)} collective-permute-done((f32[4,128,256]{2,1,0:T(8,128)S(1)}, f32[4,128,256]{2,1,0:T(8,128)S(1)}, u32[]{:S(2)}, u32[]{:S(2)}) %collective-permute-start.17) | collective-permute-done | bytes 524320 | tf_op jit(solution)/shard_map/ppermute | solution.py:35
  95.7 2.1 %collective-permute-done.16 = f32[4,128,256]{2,1,0:T(8,128)S(1)} collective-permute-done((f32[4,128,256]{2,1,0:T(8,128)S(1)}, f32[4,128,256]{2,1,0:T(8,128)S(1)}, u32[]{:S(2)}, u32[]{:S(2)}) %collective-permute-start.16) | collective-permute-done | bytes 524320 | tf_op jit(solution)/shard_map/ppermute | solution.py:35
  97.8 0.1 add_bitcast_fusion
  97.9 0.8 fusion.8
  98.7 2.9 %collective-permute-start.20 = (f32[2,128,256]{2,1,0:T(8,128)S(1)}, f32[2,128,256]{2,1,0:T(8,128)S(1)}, u32[]{:S(2)}, u32[]{:S(2)}) collective-permute-start(f32[2,128,256]{2,1,0:T(8,128)S(1)} %get-tuple-element.12), channel_id=1, source_target_pairs={{0,48},{16,0},{32,16},{48,32},{1,49},{17,1},{33,17},{49,33},{2,50}... | collective-permute-start | bytes 786440 | tf_op jit(solution)/shard_map/ppermute | solution.py:35
  101.6 0.0 collective-permute-start.18
  101.6 1.6 %collective-permute-start.19 = (f32[2,128,256]{2,1,0:T(8,128)S(1)}, f32[2,128,256]{2,1,0:T(8,128)S(1)}, u32[]{:S(2)}, u32[]{:S(2)}) collective-permute-start(f32[2,128,256]{2,1,0:T(8,128)S(1)} %get-tuple-element.15), channel_id=1, source_target_pairs={{0,32},{16,48},{32,0},{48,16},{1,33},{17,49},{33,1},{49,17},{2,34}... | collective-permute-start | bytes 786440 | tf_op jit(solution)/shard_map/ppermute | solution.py:35
  103.2 0.7 stack.95.order
  103.9 1.4 %collective-permute-done.20.refs_3_ = f32[2,128,256]{2,1,0:T(8,128)S(1)} collective-permute-done((f32[2,128,256]{2,1,0:T(8,128)S(1)}, f32[2,128,256]{2,1,0:T(8,128)S(1)}, u32[]{:S(2)}, u32[]{:S(2)}) %collective-permute-start.20) | collective-permute-done | bytes 262176 | tf_op jit(solution)/shard_map/ppermute | solution.py:35
  105.3 4.8 %collective-permute-done.18.refs_1_ = f32[2,128,256]{2,1,0:T(8,128)S(1)} collective-permute-done((f32[2,128,256]{2,1,0:T(8,128)S(1)}, f32[2,128,256]{2,1,0:T(8,128)S(1)}, u32[]{:S(2)}, u32[]{:S(2)}) %collective-permute-start.18) | collective-permute-done | bytes 262176 | tf_op jit(solution)/shard_map/ppermute | solution.py:35
  110.1 2.9 %collective-permute-done.19.refs_2_ = f32[2,128,256]{2,1,0:T(8,128)S(1)} collective-permute-done((f32[2,128,256]{2,1,0:T(8,128)S(1)}, f32[2,128,256]{2,1,0:T(8,128)S(1)}, u32[]{:S(2)}, u32[]{:S(2)}) %collective-permute-start.19) | collective-permute-done | bytes 262176 | tf_op jit(solution)/shard_map/ppermute | solution.py:35
  113.0 0.7 copy-done.3
  113.7 2.2 %shard_map.18 = f32[1,128,2048]{2,1,0:T(8,128)} custom-call(s32[8]{0:T(128)} %stack.95.order, f32[2,128,256]{2,1,0:T(8,128)} %get-tuple-element.13.refs_0_, f32[2,128,256]{2,1,0:T(8,128)} %copy-done.2, f32[2,128,256]{2,1,0:T(8,128)} %copy-done.3, f32[2,128,256]{2,1,0:T(8,128)} %copy-done.1), custom_call_target="tpu_custom_call" | custom-call | tf_op jit(solution)/shard_map/pallas_call | solution.py:119
  (11 shorter events, 0.0 us)
Async XLA Ops:
  0.0 14.5 %collective-permute-start.7 = (bf16[3,128,512]{2,1,0:T(8,128)(2,1)}, bf16[3,128,512]{2,1,0:T(8,128)(2,1)S(1)}, u32[]{:S(2)}, u32[]{:S(2)}) collective-permute-start(bf16[3,128,512]{2,1,0:T(8,128)(2,1)} %bitcast.52), channel_id=1, source_target_pairs={{0,1},{1,2},{2,3},{3,4},{4,5},{5,6},{6,7},{7,0},{64,71},{65,64},{6... | collective-permute-start | bytes 1179656 | tf_op jit(solution)/shard_map/ppermute | solution.py:35
  6.4 15.4 %collective-permute-start.8 = (bf16[3,128,512]{2,1,0:T(8,128)(2,1)}, bf16[3,128,512]{2,1,0:T(8,128)(2,1)S(1)}, u32[]{:S(2)}, u32[]{:S(2)}) collective-permute-start(bf16[3,128,512]{2,1,0:T(8,128)(2,1)} %bitcast.53), channel_id=1, source_target_pairs={{0,7},{1,0},{2,1},{3,2},{4,3},{5,4},{6,5},{7,6},{64,65},{65,66},{6... | collective-permute-start | bytes 1179656 | tf_op jit(solution)/shard_map/ppermute | solution.py:35
  6.4 15.4 %collective-permute-start = (bf16[3,128,512]{2,1,0:T(8,128)(2,1)}, bf16[3,128,512]{2,1,0:T(8,128)(2,1)S(1)}, u32[]{:S(2)}, u32[]{:S(2)}) collective-permute-start(bf16[3,128,512]{2,1,0:T(8,128)(2,1)} %bitcast.54), channel_id=1, source_target_pairs={{0,16},{16,32},{32,48},{48,0},{64,112},{80,64},{96,80},{112,96},{1... | collective-permute-start | bytes 1179656 | tf_op jit(solution)/shard_map/ppermute | solution.py:35
  14.5 8.9 %collective-permute-start.9 = (bf16[3,128,512]{2,1,0:T(8,128)(2,1)S(1)}, bf16[3,128,512]{2,1,0:T(8,128)(2,1)S(1)}, u32[]{:S(2)}, u32[]{:S(2)}) collective-permute-start(bf16[3,128,512]{2,1,0:T(8,128)(2,1)S(1)} %collective-permute-done.7.refs_9_), channel_id=1, source_target_pairs={{0,1},{1,2},{2,3},{3,4},{4,5},{5,6},{6,7},{7,0},{64,71},{65,64},{6... | collective-permute-start | bytes 1179656 | tf_op jit(solution)/shard_map/ppermute | solution.py:35
  17.8 10.9 %collective-permute-start.3 = (bf16[3,128,512]{2,1,0:T(8,128)(2,1)}, bf16[3,128,512]{2,1,0:T(8,128)(2,1)S(1)}, u32[]{:S(2)}, u32[]{:S(2)}) collective-permute-start(bf16[3,128,512]{2,1,0:T(8,128)(2,1)} %bitcast.55), channel_id=1, source_target_pairs={{0,8},{8,0},{1,9},{9,1},{2,10},{10,2},{3,11},{11,3},{4,12},{12,4},... | collective-permute-start | bytes 1179656 | tf_op jit(solution)/shard_map/ppermute | solution.py:35
  20.6 9.4 %collective-permute-start.1 = (bf16[3,128,512]{2,1,0:T(8,128)(2,1)}, bf16[3,128,512]{2,1,0:T(8,128)(2,1)S(1)}, u32[]{:S(2)}, u32[]{:S(2)}) collective-permute-start(bf16[3,128,512]{2,1,0:T(8,128)(2,1)} %bitcast.56), channel_id=1, source_target_pairs={{0,48},{16,0},{32,16},{48,32},{64,80},{80,96},{96,112},{112,64},{1... | collective-permute-start | bytes 1179656 | tf_op jit(solution)/shard_map/ppermute | solution.py:35
  21.9 10.1 %collective-permute-start.10 = (bf16[3,128,512]{2,1,0:T(8,128)(2,1)S(1)}, bf16[3,128,512]{2,1,0:T(8,128)(2,1)S(1)}, u32[]{:S(2)}, u32[]{:S(2)}) collective-permute-start(bf16[3,128,512]{2,1,0:T(8,128)(2,1)S(1)} %collective-permute-done.8.refs_10_), channel_id=1, source_target_pairs={{0,7},{1,0},{2,1},{3,2},{4,3},{5,4},{6,5},{7,6},{64,65},{65,66},{6... | collective-permute-start | bytes 1179656 | tf_op jit(solution)/shard_map/ppermute | solution.py:35
  21.9 10.1 %collective-permute-start.2 = (bf16[3,128,512]{2,1,0:T(8,128)(2,1)S(1)}, bf16[3,128,512]{2,1,0:T(8,128)(2,1)S(1)}, u32[]{:S(2)}, u32[]{:S(2)}) collective-permute-start(bf16[3,128,512]{2,1,0:T(8,128)(2,1)S(1)} %collective-permute-done.refs_1_), channel_id=1, source_target_pairs={{0,16},{16,32},{32,48},{48,0},{64,112},{80,64},{96,80},{112,96},{1... | collective-permute-start | bytes 1179656 | tf_op jit(solution)/shard_map/ppermute | solution.py:35
  23.4 11.1 %collective-permute-start.11 = (bf16[3,128,512]{2,1,0:T(8,128)(2,1)S(1)}, bf16[3,128,512]{2,1,0:T(8,128)(2,1)S(1)}, u32[]{:S(2)}, u32[]{:S(2)}) collective-permute-start(bf16[3,128,512]{2,1,0:T(8,128)(2,1)S(1)} %collective-permute-done.9.refs_11_), channel_id=1, source_target_pairs={{0,1},{1,2},{2,3},{3,4},{4,5},{5,6},{6,7},{7,0},{64,71},{65,64},{6... | collective-permute-start | bytes 1179656 | tf_op jit(solution)/shard_map/ppermute | solution.py:35
  28.7 12.4 %collective-permute-start.5 = (bf16[3,128,512]{2,1,0:T(8,128)(2,1)S(1)}, bf16[3,128,512]{2,1,0:T(8,128)(2,1)}, u32[]{:S(2)}, u32[]{:S(2)}) collective-permute-start(bf16[3,128,512]{2,1,0:T(8,128)(2,1)S(1)} %collective-permute-done.3.refs_4_), channel_id=1, source_target_pairs={{0,48},{16,0},{32,16},{48,32},{64,80},{80,96},{96,112},{112,64},{1... | collective-permute-start | bytes 1179656 | tf_op jit(solution)/shard_map/ppermute | solution.py:35
  30.0 11.1 %collective-permute-start.4 = (bf16[3,128,512]{2,1,0:T(8,128)(2,1)S(1)}, bf16[3,128,512]{2,1,0:T(8,128)(2,1)}, u32[]{:S(2)}, u32[]{:S(2)}) collective-permute-start(bf16[3,128,512]{2,1,0:T(8,128)(2,1)S(1)} %collective-permute-done.3.refs_4_), channel_id=1, source_target_pairs={{0,16},{16,32},{32,48},{48,0},{64,112},{80,64},{96,80},{112,96},{1... | collective-permute-start | bytes 1179656 | tf_op jit(solution)/shard_map/ppermute | solution.py:35
  31.9 9.1 %collective-permute-start.12 = (bf16[3,128,512]{2,1,0:T(8,128)(2,1)S(1)}, bf16[3,128,512]{2,1,0:T(8,128)(2,1)}, u32[]{:S(2)}, u32[]{:S(2)}) collective-permute-start(bf16[3,128,512]{2,1,0:T(8,128)(2,1)S(1)} %collective-permute-done.10.refs_12_), channel_id=1, source_target_pairs={{0,7},{1,0},{2,1},{3,2},{4,3},{5,4},{6,5},{7,6},{64,65},{65,66},{6... | collective-permute-start | bytes 1179656 | tf_op jit(solution)/shard_map/ppermute | solution.py:35
  31.9 9.1 %collective-permute-start.6 = (bf16[3,128,512]{2,1,0:T(8,128)(2,1)S(1)}, bf16[3,128,512]{2,1,0:T(8,128)(2,1)}, u32[]{:S(2)}, u32[]{:S(2)}) collective-permute-start(bf16[3,128,512]{2,1,0:T(8,128)(2,1)S(1)} %collective-permute-done.2.refs_3_), channel_id=1, source_target_pairs={{0,8},{8,0},{1,9},{9,1},{2,10},{10,2},{3,11},{11,3},{4,12},{12,4},... | collective-permute-start | bytes 1179656 | tf_op jit(solution)/shard_map/ppermute | solution.py:35
  34.5 11.9 %collective-permute-start.13 = (bf16[3,128,512]{2,1,0:T(8,128)(2,1)S(1)}, bf16[3,128,512]{2,1,0:T(8,128)(2,1)}, u32[]{:S(2)}, u32[]{:S(2)}) collective-permute-start(bf16[3,128,512]{2,1,0:T(8,128)(2,1)S(1)} %collective-permute-done.11.refs_13_), channel_id=1, source_target_pairs={{0,1},{1,2},{2,3},{3,4},{4,5},{5,6},{6,7},{7,0},{64,71},{65,64},{6... | collective-permute-start | bytes 1179656 | tf_op jit(solution)/shard_map/ppermute | solution.py:35
  46.3 1.0 copy-start
  62.9 5.0 %collective-permute-start.14 = (f32[2,8,128,256]{3,2,1,0:T(8,128)S(1)}, f32[2,8,128,256]{3,2,1,0:T(8,128)S(1)}, u32[]{:S(2)}, u32[]{:S(2)}) collective-permute-start(f32[2,8,128,256]{3,2,1,0:T(8,128)S(1)} %get-tuple-element.8), channel_id=1, source_target_pairs={{0,64},{64,0},{1,65},{65,1},{2,66},{66,2},{3,67},{67,3},{4,68},{68... | collective-permute-start | bytes 6291464 | tf_op jit(solution)/shard_map/ppermute | solution.py:35
  68.3 13.2 %collective-permute-start.15 = (f32[4,128,256]{2,1,0:T(8,128)S(1)}, f32[4,128,256]{2,1,0:T(8,128)S(1)}, u32[]{:S(2)}, u32[]{:S(2)}) collective-permute-start(f32[4,128,256]{2,1,0:T(8,128)S(1)} %get-tuple-element.11), channel_id=1, source_target_pairs={{0,128},{128,0},{1,129},{129,1},{2,130},{130,2},{3,131},{131,3},{4... | collective-permute-start | bytes 1572872 | tf_op jit(solution)/shard_map/ppermute | solution.py:35
  68.6 27.1 %collective-permute-start.17 = (f32[4,128,256]{2,1,0:T(8,128)S(1)}, f32[4,128,256]{2,1,0:T(8,128)S(1)}, u32[]{:S(2)}, u32[]{:S(2)}) collective-permute-start(f32[4,128,256]{2,1,0:T(8,128)S(1)} %get-tuple-element.9), channel_id=1, source_target_pairs={{0,8},{8,0},{1,9},{9,1},{2,10},{10,2},{3,11},{11,3},{4,12},{12,4},... | collective-permute-start | bytes 1572872 | tf_op jit(solution)/shard_map/ppermute | solution.py:35
  72.6 25.3 %collective-permute-start.16 = (f32[4,128,256]{2,1,0:T(8,128)S(1)}, f32[4,128,256]{2,1,0:T(8,128)S(1)}, u32[]{:S(2)}, u32[]{:S(2)}) collective-permute-start(f32[4,128,256]{2,1,0:T(8,128)S(1)} %get-tuple-element.10), channel_id=1, source_target_pairs={{0,136},{8,128},{128,8},{136,0},{1,137},{9,129},{129,9},{137,1},{2... | collective-permute-start | bytes 1572872 | tf_op jit(solution)/shard_map/ppermute | solution.py:35
  98.7 6.6 %collective-permute-start.20 = (f32[2,128,256]{2,1,0:T(8,128)S(1)}, f32[2,128,256]{2,1,0:T(8,128)S(1)}, u32[]{:S(2)}, u32[]{:S(2)}) collective-permute-start(f32[2,128,256]{2,1,0:T(8,128)S(1)} %get-tuple-element.12), channel_id=1, source_target_pairs={{0,48},{16,0},{32,16},{48,32},{1,49},{17,1},{33,17},{49,33},{2,50}... | collective-permute-start | bytes 786440 | tf_op jit(solution)/shard_map/ppermute | solution.py:35
  101.6 8.5 %collective-permute-start.18 = (f32[2,128,256]{2,1,0:T(8,128)S(1)}, f32[2,128,256]{2,1,0:T(8,128)S(1)}, u32[]{:S(2)}, u32[]{:S(2)}) collective-permute-start(f32[2,128,256]{2,1,0:T(8,128)S(1)} %get-tuple-element.14), channel_id=1, source_target_pairs={{0,16},{16,32},{32,48},{48,0},{1,17},{17,33},{33,49},{49,1},{2,18}... | collective-permute-start | bytes 786440 | tf_op jit(solution)/shard_map/ppermute | solution.py:35
  101.6 11.5 %collective-permute-start.19 = (f32[2,128,256]{2,1,0:T(8,128)S(1)}, f32[2,128,256]{2,1,0:T(8,128)S(1)}, u32[]{:S(2)}, u32[]{:S(2)}) collective-permute-start(f32[2,128,256]{2,1,0:T(8,128)S(1)} %get-tuple-element.15), channel_id=1, source_target_pairs={{0,32},{16,48},{32,0},{48,16},{1,33},{17,49},{33,1},{49,17},{2,34}... | collective-permute-start | bytes 786440 | tf_op jit(solution)/shard_map/ppermute | solution.py:35
  105.3 7.7 %copy-start.1 = (f32[2,128,256]{2,1,0:T(8,128)}, f32[2,128,256]{2,1,0:T(8,128)S(1)}, u32[]{:S(2)}) copy-start(f32[2,128,256]{2,1,0:T(8,128)S(1)} %collective-permute-done.20.refs_3_) | copy-start | bytes 786436
  110.1 2.9 %copy-start.2 = (f32[2,128,256]{2,1,0:T(8,128)}, f32[2,128,256]{2,1,0:T(8,128)S(1)}, u32[]{:S(2)}) copy-start(f32[2,128,256]{2,1,0:T(8,128)S(1)} %collective-permute-done.18.refs_1_) | copy-start | bytes 786436
  113.0 0.7 copy-start.3

commit v3 on v2

v3 whole, which is shorter than its diff:
```python
import functools

import jax
import jax.numpy as jnp
from jax import lax
from jax.experimental import pallas as pl
from jax.experimental.pallas import tpu as pltpu
from jax.sharding import Mesh, PartitionSpec as P

XL, CORE, Y, XH, Z = 2, 2, 4, 2, 8
AXES = ("xl", "core", "y", "xh", "z")


def split_mesh(mesh):
    return Mesh(mesh.devices.reshape(XL, CORE, Y, XH, Z), AXES)


def move(value, axes, target):
    sizes = {"xl": XL, "core": CORE, "y": Y, "xh": XH, "z": Z}
    dims = [sizes[a] for a in axes]
    count = 1
    for d in dims:
        count *= d
    pairs = []
    for source in range(count):
        rest, place = source, []
        for d in reversed(dims):
            place.insert(0, rest % d)
            rest //= d
        goal = target(*place)
        flat = 0
        for d, g in zip(dims, goal):
            flat = flat * d + g % d
        pairs.append((source, flat))
    return lax.ppermute(value, axes, pairs)


def along_z(value, step):
    return move(value, ("z",), lambda z: (z + step,))


def turn(core, step):
    return step if core == 0 else -step


def along_y(value, step):
    return move(value, ("core", "y"), lambda c, y: (c, y + turn(c, step)))


def across(value):
    return move(value, ("xh",), lambda h: (h + 1,))


def product_kernel(count, order, *refs):
    row_blocks, column_blocks = refs[:count], refs[count : count + 4]
    send, keep, rows, columns, row_sem, column_sem = refs[count + 4 :]
    aux, height, occ = row_blocks[0].shape
    sub = height // 4
    copies = []
    for k in range(4):
        for slot in range(4):
            copies.append(
                pltpu.make_async_copy(
                    column_blocks[k].at[:, pl.ds(pl.multiple_of(order[16 + slot] * sub, sub), sub), :],
                    columns.at[slot // 2, :, pl.ds(pl.multiple_of((slot % 2) * height + order[8 + k] * sub, sub), sub), :],
                    column_sem.at[k * 4 + slot],
                )
            )
    for k in range(count):
        place = pl.multiple_of(order[k] * height, height)
        copies.append(pltpu.make_async_copy(row_blocks[k], rows.at[:, pl.ds(place, height), :], row_sem.at[k]))
    for c in copies:
        c.start()
    for c in copies:
        c.wait()
    for half, target in enumerate((send, keep)):
        total = None
        for a in range(aux):
            part = lax.dot_general(
                rows[a], columns[half, a], (((1,), (1,)), ((), ())), preferred_element_type=jnp.float32
            )
            total = part if total is None else total + part
        for side in range(2):
            target[side] = total[:, side * height : (side + 1) * height]


def products(order, row_blocks, column_blocks):
    aux, height, occ = row_blocks[0].shape
    count = len(row_blocks)
    shape = jax.ShapeDtypeStruct((2, count * height, height), jnp.float32)
    return pl.pallas_call(
        functools.partial(product_kernel, count),
        out_shape=[shape, shape],
        in_specs=[pl.BlockSpec(memory_space=pltpu.SMEM)] + [pl.BlockSpec(memory_space=pl.ANY)] * (count + 4),
        out_specs=[pl.BlockSpec(memory_space=pltpu.VMEM)] * 2,
        scratch_shapes=[
            pltpu.VMEM((aux, count * height, occ), jnp.bfloat16),
            pltpu.VMEM((2, aux, 2 * height, occ), jnp.bfloat16),
            pltpu.SemaphoreType.DMA((count,)),
            pltpu.SemaphoreType.DMA((16,)),
        ],
        compiler_params=pltpu.CompilerParams(vmem_limit_bytes=32 * 1024 * 1024),
        cost_estimate=pl.CostEstimate(
            flops=2 * count * height * 4 * height * aux * occ, bytes_accessed=(count + 4) * aux * height * occ * 2, transcendentals=0
        ),
    )(order, *row_blocks, *column_blocks)


def assemble_kernel(order, *refs):
    out = refs[-1]
    height = out.shape[1]
    group = lax.broadcasted_iota(jnp.int32, (height, height), 1) // (height // 4)
    start = order[8]
    block = lax.rem(start + lax.rem(group - start + 8, 4), 8)
    low = block < 4
    for d in range(4):
        for h in range(2):
            first = pl.multiple_of(order[2 * d + h] * (2 * height), 2 * height)
            zero, one = refs[d][h], refs[4 + d][h]
            out[0, :, pl.ds(first, height)] = jnp.where(low, zero, one)
            out[0, :, pl.ds(first + height, height)] = jnp.where(low, one, zero)


def assemble(order, pieces):
    height = pieces[0].shape[1]
    return pl.pallas_call(
        assemble_kernel,
        out_shape=jax.ShapeDtypeStruct((1, height, 16 * height), jnp.float32),
        in_specs=[pl.BlockSpec(memory_space=pltpu.SMEM)] + [pl.BlockSpec(memory_space=pltpu.VMEM)] * 8,
        out_specs=pl.BlockSpec(memory_space=pltpu.VMEM),
    )(order, *pieces)


def swap_cores(send, keep):
    arrived = move(send, ("core",), lambda c: (c + 1,))
    return [keep[side] + arrived[side] for side in range(2)]


def split4(value):
    return value.reshape(4, value.shape[0] // 4, value.shape[1])


def per_device(factors):
    own = jnp.transpose(factors, (1, 0, 2))
    xl, core, y, xh, z = (lax.axis_index(a) for a in AXES)
    sign = 1 - 2 * core

    za1 = along_z(own, 1)
    zb1 = along_z(own, -1)
    ya1 = along_y(own, 1)
    yb1 = along_y(own, -1)
    x0 = across(own)
    za2 = along_z(za1, 1)
    zb2 = along_z(zb1, -1)
    ya2 = along_y(ya1, 1)
    xa1 = along_y(x0, 1)
    xb1 = along_y(x0, -1)
    za3 = along_z(za2, 1)
    zb3 = along_z(zb2, -1)
    xa2 = across(ya2)
    far_z = jnp.where(core == 0, za3, zb3)
    z4 = move(far_z, ("core", "z"), lambda c, k: (c, k + turn(c, 1)))

    dy = [0, -sign, sign, 2]
    row_order = [lax.rem(d + 4, 4) for d in dy]
    fit_order = [
        (1 - xl) * 2 + 1 - core,
        xl * 2 + 1 - core,
        (1 - xl) * 2 + core,
        xl * 2 + core,
    ]
    rows = [[own, ya1, yb1, ya2], [x0, xa1, xb1, xa2]]
    columns = [[own, za1, zb1, za2], [zb2, za3, zb3, z4]]
    shifts = [[0, -1, 1, -2], [2, -3, 3, 4]]

    def order(half):
        column_order = [lax.rem(z + d + 8, 4) for d in shifts[half]]
        values = row_order + [v + 4 for v in row_order] + column_order + [0] * 4 + fit_order
        return jnp.stack([jnp.int32(v) for v in values])

    sums = []
    for half in range(2):
        table = order(half)
        other0, mine0 = swap_cores(*products(table, rows[0], columns[half]))
        other1, mine1 = swap_cores(*products(table, rows[1], columns[half]))
        near = move(other0, ("xl",), lambda a: (a + 1,))
        cross = move(other1, ("xl", "xh"), lambda a, h: (a + 1, h + 1))
        far = across(mine1)
        sums.append(jnp.stack([split4(mine0 + near), split4(cross + far)], axis=1))

    pieces = []
    for half in range(2):
        t = sums[half]
        pieces += [t[0]] + [move(t[d], ("y",), lambda b, d=d: (b + d,)) for d in range(1, 4)]
    places = [lax.rem(y - d + 4, 4) * 2 + lax.rem(xh + h, 2) for d in range(4) for h in range(2)]
    places.append(lax.rem(z + 6, 8))
    return assemble(jnp.stack(places).astype(jnp.int32), pieces)


def solution(mesh):
    return jax.shard_map(
        per_device,
        mesh=split_mesh(mesh),
        in_specs=(P(("y", "xh", "z"), ("xl", "core"), None),),
        out_specs=P(("xl", "core"), ("y", "xh", "z"), None),
        check_vma=False,
    )
```

time: 117 us -> 104 us (0.89)
  waiting for transfers between devices: 54.5 us -> 27.9 us
  starting transfers between devices: 39.8 us -> 45.8 us
  other arithmetic: 1.19 us -> 5.55 us
  local copies, waits for them, and re-layouts: 2.63 us -> 4.55 us
    ppermute x21 -> x30, waiting for transfers between devices: 54.5 us -> 27.9 us  [move(): return lax.ppermute(value, axes, pairs)]
    ppermute x21 -> x30, starting transfers between devices: 39.8 us -> 45.8 us  [move(): return lax.ppermute(value, axes, pairs)]
    add x1 -> x8, other arithmetic: 0.28 us -> 3.4 us  [the longest x4 2.29 us: swap_cores(): return [keep[side] + arrived[side] for side in range(2)]]
    unnamed x8 -> x28, local copies, waits for them, and re-layouts: 1.7 us -> 3.7 us
    pallas_call x1 -> x4, Pallas kernels: 15.6 us -> 15.6 us  [products(): pl.pallas_call(functools.partial(product_kernel, count), out_shape=[shape...]
  transfers between devices with their start and end apart: 21 -> 30, of which waited for: 11 -> 8; matrix products, arithmetic and copies ran while one was open for 1% -> 6% of each run, Pallas kernels for 0% -> 15%
where the time goes in v3:
time: 104 us; the launch traced here: 102 us
  starting transfers between devices  45.8 us (44%)
  waiting for transfers between devices  27.9 us (27%)
  Pallas kernels  18 us (17%)
  other arithmetic  5.55 us (5%)
  local copies, waits for them, and re-layouts  4.55 us (4%)
    ppermute x30, starting transfers between devices, move(): return lax.ppermute(value, axes, pairs)  45.8 us
    ppermute x30, waiting for transfers between devices, move(): return lax.ppermute(value, axes, pairs)  27.9 us
    pallas_call x4, Pallas kernels, products(): pl.pallas_call(functools.partial(product_kernel, count), out_shape=[shape...  15.6 us
    unnamed x28, local copies, waits for them, and re-layouts  3.7 us
    pallas_call x1, Pallas kernels, assemble(): pl.pallas_call(assemble_kernel, out_shape=jax.ShapeDtypeStruct((1, height...  2.38 us
    add x4, other arithmetic, swap_cores(): return [keep[side] + arrived[side] for side in range(2)]  2.29 us
  transfers between devices with their start and end apart: 30, of which 8 were waited for; matrix products, arithmetic and copies ran while one was open for 6% of the time, Pallas kernels for 15%

profile of v3, /device:TPU:1, one launch (start us, length us, event | category | flops | bytes accessed | tf_op | source)
XLA Modules:
  0.0 102.0 jit_solution(410992782048561756)
XLA Ops:
  0.0 2.5 %collective-permute-start.3 = (bf16[3,128,512]{2,1,0:T(8,128)(2,1)}, bf16[3,128,512]{2,1,0:T(8,128)(2,1)S(1)}, u32[]{:S(2)}, u32[]{:S(2)}) collective-permute-start(bf16[3,128,512]{2,1,0:T(8,128)(2,1)} %bitcast.66), channel_id=1, source_target_pairs={{0,1},{1,2},{2,3},{3,4},{4,5},{5,6},{6,7},{7,0},{8,9},{9,10},{10,1... | collective-permute-start | bytes 1179656 | tf_op jit(solution)/shard_map/ppermute | solution.py:35
  2.5 3.9 %collective-permute-start.4 = (bf16[3,128,512]{2,1,0:T(8,128)(2,1)}, bf16[3,128,512]{2,1,0:T(8,128)(2,1)S(1)}, u32[]{:S(2)}, u32[]{:S(2)}) collective-permute-start(bf16[3,128,512]{2,1,0:T(8,128)(2,1)} %bitcast.67), channel_id=1, source_target_pairs={{0,7},{1,0},{2,1},{3,2},{4,3},{5,4},{6,5},{7,6},{8,15},{9,8},{10,9... | collective-permute-start | bytes 1179656 | tf_op jit(solution)/shard_map/ppermute | solution.py:35
  6.4 2.7 %collective-permute-start = (bf16[3,128,512]{2,1,0:T(8,128)(2,1)}, bf16[3,128,512]{2,1,0:T(8,128)(2,1)S(1)}, u32[]{:S(2)}, u32[]{:S(2)}) collective-permute-start(bf16[3,128,512]{2,1,0:T(8,128)(2,1)} %bitcast.68), channel_id=1, source_target_pairs={{0,16},{16,32},{32,48},{48,0},{64,112},{80,64},{96,80},{112,96},{1... | collective-permute-start | bytes 1179656 | tf_op jit(solution)/shard_map/ppermute | solution.py:35
  9.1 6.3 %collective-permute-done.3.refs_5_ = bf16[3,128,512]{2,1,0:T(8,128)(2,1)S(1)} collective-permute-done((bf16[3,128,512]{2,1,0:T(8,128)(2,1)}, bf16[3,128,512]{2,1,0:T(8,128)(2,1)S(1)}, u32[]{:S(2)}, u32[]{:S(2)}) %collective-permute-start.3) | collective-permute-done | bytes 393248 | tf_op jit(solution)/shard_map/ppermute | solution.py:35
  15.5 2.7 %collective-permute-start.18 = (bf16[3,128,512]{2,1,0:T(8,128)(2,1)S(1)}, bf16[3,128,512]{2,1,0:T(8,128)(2,1)S(1)}, u32[]{:S(2)}, u32[]{:S(2)}) collective-permute-start(bf16[3,128,512]{2,1,0:T(8,128)(2,1)S(1)} %collective-permute-done.4.refs_6_), channel_id=1, source_target_pairs={{0,7},{1,0},{2,1},{3,2},{4,3},{5,4},{6,5},{7,6},{8,15},{9,8},{10,9... | collective-permute-start | bytes 1179656 | tf_op jit(solution)/shard_map/ppermute | solution.py:35
  18.1 2.7 %collective-permute-start.8 = (bf16[3,128,512]{2,1,0:T(8,128)(2,1)}, bf16[3,128,512]{2,1,0:T(8,128)(2,1)S(1)}, u32[]{:S(2)}, u32[]{:S(2)}) collective-permute-start(bf16[3,128,512]{2,1,0:T(8,128)(2,1)} %bitcast.69), channel_id=1, source_target_pairs={{0,8},{8,0},{1,9},{9,1},{2,10},{10,2},{3,11},{11,3},{4,12},{12,4},... | collective-permute-start | bytes 1179656 | tf_op jit(solution)/shard_map/ppermute | solution.py:35
  20.9 1.3 %collective-permute-start.1 = (bf16[3,128,512]{2,1,0:T(8,128)(2,1)}, bf16[3,128,512]{2,1,0:T(8,128)(2,1)S(1)}, u32[]{:S(2)}, u32[]{:S(2)}) collective-permute-start(bf16[3,128,512]{2,1,0:T(8,128)(2,1)} %bitcast.70), channel_id=1, source_target_pairs={{0,48},{16,0},{32,16},{48,32},{64,80},{80,96},{96,112},{112,64},{1... | collective-permute-start | bytes 1179656 | tf_op jit(solution)/shard_map/ppermute | solution.py:35
  22.2 1.4 %collective-permute-start.2 = (bf16[3,128,512]{2,1,0:T(8,128)(2,1)S(1)}, bf16[3,128,512]{2,1,0:T(8,128)(2,1)S(1)}, u32[]{:S(2)}, u32[]{:S(2)}) collective-permute-start(bf16[3,128,512]{2,1,0:T(8,128)(2,1)S(1)} %collective-permute-done.refs_1_), channel_id=1, source_target_pairs={{0,16},{16,32},{32,48},{48,0},{64,112},{80,64},{96,80},{112,96},{1... | collective-permute-start | bytes 1179656 | tf_op jit(solution)/shard_map/ppermute | solution.py:35
  23.6 2.5 %collective-permute-done.5.refs_7_ = bf16[3,128,512]{2,1,0:T(8,128)(2,1)} collective-permute-done((bf16[3,128,512]{2,1,0:T(8,128)(2,1)S(1)}, bf16[3,128,512]{2,1,0:T(8,128)(2,1)}, u32[]{:S(2)}, u32[]{:S(2)}) %collective-permute-start.5) | collective-permute-done | bytes 393248 | tf_op jit(solution)/shard_map/ppermute | solution.py:35
  26.2 2.7 %collective-permute-start.20 = (bf16[3,128,512]{2,1,0:T(8,128)(2,1)S(1)}, bf16[3,128,512]{2,1,0:T(8,128)(2,1)S(1)}, u32[]{:S(2)}, u32[]{:S(2)}) collective-permute-start(bf16[3,128,512]{2,1,0:T(8,128)(2,1)S(1)} %collective-permute-done.18.refs_4_), channel_id=1, source_target_pairs={{0,7},{1,0},{2,1},{3,2},{4,3},{5,4},{6,5},{7,6},{8,15},{9,8},{10,9... | collective-permute-start | bytes 1179656 | tf_op jit(solution)/shard_map/ppermute | solution.py:35
  28.9 2.8 %collective-permute-start.9 = (bf16[3,128,512]{2,1,0:T(8,128)(2,1)S(1)}, bf16[3,128,512]{2,1,0:T(8,128)(2,1)}, u32[]{:S(2)}, u32[]{:S(2)}) collective-permute-start(bf16[3,128,512]{2,1,0:T(8,128)(2,1)S(1)} %collective-permute-done.8.refs_0_), channel_id=1, source_target_pairs={{0,16},{16,32},{32,48},{48,0},{64,112},{80,64},{96,80},{112,96},{1... | collective-permute-start | bytes 1179656 | tf_op jit(solution)/shard_map/ppermute | solution.py:35
  31.8 2.8 %collective-permute-start.11 = (bf16[3,128,512]{2,1,0:T(8,128)(2,1)S(1)}, bf16[3,128,512]{2,1,0:T(8,128)(2,1)}, u32[]{:S(2)}, u32[]{:S(2)}) collective-permute-start(bf16[3,128,512]{2,1,0:T(8,128)(2,1)S(1)} %collective-permute-done.2.refs_3_), channel_id=1, source_target_pairs={{0,8},{8,0},{1,9},{9,1},{2,10},{10,2},{3,11},{11,3},{4,12},{12,4},... | collective-permute-start | bytes 1179656 | tf_op jit(solution)/shard_map/ppermute | solution.py:35
  34.6 1.0 copy-done
  35.6 4.1 %shard_map.17 = (f32[2,512,128]{2,1,0:T(8,128)}, f32[2,512,128]{2,1,0:T(8,128)S(1)}) custom-call(s32[20]{0:T(128)S(1)} %stack.120.order, bf16[3,128,512]{2,1,0:T(8,128)(2,1)S(1)} %bitcast.71, bf16[3,128,512]{2,1,0:T(8,128)(2,1)S(1)} %collective-permute-done.refs_1_, bf16[3,128,512]{2,1,0:T(8,128)(2,1)S(1)} %collective-permute-done.1.refs_2_, ...), custom_call_target="tpu_custom_call" | custom-call | flops 805306368 | bytes 3145728 | tf_op jit(solution)/shard_map/pallas_call | solution.py:91
  39.7 0.8 copy-done.6
  40.5 3.4 %collective-permute-start.6 = (f32[2,512,128]{2,1,0:T(8,128)}, f32[2,512,128]{2,1,0:T(8,128)}, u32[]{:S(2)}, u32[]{:S(2)}) collective-permute-start(f32[2,512,128]{2,1,0:T(8,128)} %get-tuple-element.14), channel_id=1, source_target_pairs={{0,64},{64,0},{1,65},{65,1},{2,66},{66,2},{3,67},{67,3},{4,68},{68... | collective-permute-start | bytes 1572872 | tf_op jit(solution)/shard_map/ppermute | solution.py:35
  43.9 0.8 broadcast_select_fusion
  44.7 0.3 copy-done.1
  45.0 0.1 copy-done.3
  45.2 4.5 %shard_map.18 = (f32[2,512,128]{2,1,0:T(8,128)}, f32[2,512,128]{2,1,0:T(8,128)S(1)}) custom-call(s32[20]{0:T(128)S(1)} %stack.120.order, bf16[3,128,512]{2,1,0:T(8,128)(2,1)S(1)} %collective-permute-done.8.refs_0_, bf16[3,128,512]{2,1,0:T(8,128)(2,1)} %collective-permute-done.9.refs_1_, bf16[3,128,512]{2,1,0:T(8,128)(2,1)} %collective-permute-done.10.refs_2_, ...), custom_call_target="tpu_custom_call" | custom-call | flops 805306368 | bytes 3145728 | tf_op jit(solution)/shard_map/pallas_call | solution.py:91
  49.7 0.8 copy-done.4
  50.5 1.1 %collective-permute-start.12 = (f32[2,512,128]{2,1,0:T(8,128)}, f32[2,512,128]{2,1,0:T(8,128)}, u32[]{:S(2)}, u32[]{:S(2)}) collective-permute-start(f32[2,512,128]{2,1,0:T(8,128)} %get-tuple-element.16), channel_id=1, source_target_pairs={{0,64},{64,0},{1,65},{65,1},{2,66},{66,2},{3,67},{67,3},{4,68},{68... | collective-permute-start | bytes 1572872 | tf_op jit(solution)/shard_map/ppermute | solution.py:35
  51.7 1.1 %fusion.7 = f32[512,128]{1,0:T(8,128)S(1)} fusion(f32[2,512,128]{2,1,0:T(8,128)} %collective-permute-done.6, f32[2,512,128]{2,1,0:T(8,128)} %copy-done.6), kind=kLoop, calls=%fused_computation.27 | loop fusion | flops 65536 | bytes 786432 | tf_op jit(solution)/shard_map/add | solution.py:136
  52.7 0.2 collective-permute-start.7
  52.9 3.3 %shard_map.19 = (f32[2,512,128]{2,1,0:T(8,128)S(1)}, f32[2,512,128]{2,1,0:T(8,128)S(1)}) custom-call(s32[20]{0:T(128)S(1)} %stack.126.order, bf16[3,128,512]{2,1,0:T(8,128)(2,1)S(1)} %bitcast.74, bf16[3,128,512]{2,1,0:T(8,128)(2,1)S(1)} %collective-permute-done.refs_1_, bf16[3,128,512]{2,1,0:T(8,128)(2,1)S(1)} %collective-permute-done.1.refs_2_, ...), custom_call_target="tpu_custom_call" | custom-call | flops 805306368 | bytes 3145728 | tf_op jit(solution)/shard_map/pallas_call | solution.py:91
  56.2 1.2 %collective-permute-start.22 = (f32[2,512,128]{2,1,0:T(8,128)S(1)}, f32[2,512,128]{2,1,0:T(8,128)S(1)}, u32[]{:S(2)}, u32[]{:S(2)}) collective-permute-start(f32[2,512,128]{2,1,0:T(8,128)S(1)} %get-tuple-element.18), channel_id=1, source_target_pairs={{0,64},{64,0},{1,65},{65,1},{2,66},{66,2},{3,67},{67,3},{4,68},{68... | collective-permute-start | bytes 1572872 | tf_op jit(solution)/shard_map/ppermute | solution.py:35
  57.4 3.7 %shard_map.20 = (f32[2,512,128]{2,1,0:T(8,128)S(1)}, f32[2,512,128]{2,1,0:T(8,128)S(1)}) custom-call(s32[20]{0:T(128)S(1)} %stack.126.order, bf16[3,128,512]{2,1,0:T(8,128)(2,1)S(1)} %collective-permute-done.8.refs_0_, bf16[3,128,512]{2,1,0:T(8,128)(2,1)} %collective-permute-done.9.refs_1_, bf16[3,128,512]{2,1,0:T(8,128)(2,1)} %collective-permute-done.10.refs_2_, ...), custom_call_target="tpu_custom_call" | custom-call | flops 805306368 | bytes 3145728 | tf_op jit(solution)/shard_map/pallas_call | solution.py:91
  61.1 0.1 collective-permute-start.24
  61.3 1.1 %fusion.5 = (f32[512,128]{1,0:T(8,128)S(1)}, f32[512,128]{1,0:T(8,128)S(1)}) fusion(f32[2,512,128]{2,1,0:T(8,128)} %collective-permute-done.12, f32[2,512,128]{2,1,0:T(8,128)S(1)} %copy-done.5), kind=kLoop, calls=%fused_computation.23 | loop fusion | flops 131072 | bytes 1572864 | tf_op jit(solution)/shard_map/add | solution.py:136
  62.4 1.7 %collective-permute-start.13 = (f32[512,128]{1,0:T(8,128)S(1)}, f32[512,128]{1,0:T(8,128)S(1)}, u32[]{:S(2)}, u32[]{:S(2)}) collective-permute-start(f32[512,128]{1,0:T(8,128)S(1)} %get-tuple-element.24), channel_id=1, source_target_pairs={{0,136},{8,128},{128,8},{136,0},{1,137},{9,129},{129,9},{137,1},{2... | collective-permute-start | bytes 786440 | tf_op jit(solution)/shard_map/ppermute | solution.py:35
  64.2 0.9 collective-permute-start.14
  65.0 1.0 fusion.9
  66.0 10.7 %collective-permute-done.13 = f32[512,128]{1,0:T(8,128)S(1)} collective-permute-done((f32[512,128]{1,0:T(8,128)S(1)}, f32[512,128]{1,0:T(8,128)S(1)}, u32[]{:S(2)}, u32[]{:S(2)}) %collective-permute-start.13) | collective-permute-done | bytes 262176 | tf_op jit(solution)/shard_map/ppermute | solution.py:35
  77.0 1.7 %collective-permute-start.25 = (f32[512,128]{1,0:T(8,128)S(1)}, f32[512,128]{1,0:T(8,128)S(1)}, u32[]{:S(2)}, u32[]{:S(2)}) collective-permute-start(f32[512,128]{1,0:T(8,128)S(1)} %get-tuple-element.22), channel_id=1, source_target_pairs={{0,136},{8,128},{128,8},{136,0},{1,137},{9,129},{129,9},{137,1},{2... | collective-permute-start | bytes 786440 | tf_op jit(solution)/shard_map/ppermute | solution.py:35
  78.7 1.6 %collective-permute-start.26 = (f32[512,128]{1,0:T(8,128)S(1)}, f32[512,128]{1,0:T(8,128)S(1)}, u32[]{:S(2)}, u32[]{:S(2)}) collective-permute-start(f32[512,128]{1,0:T(8,128)S(1)} %get-tuple-element.21), channel_id=1, source_target_pairs={{0,8},{8,0},{1,9},{9,1},{2,10},{10,2},{3,11},{11,3},{4,12},{12,4},... | collective-permute-start | bytes 786440 | tf_op jit(solution)/shard_map/ppermute | solution.py:35
  80.3 0.7 fusion.23
  81.1 3.1 %collective-permute-start.16 = (f32[2,128,128]{2,1,0:T(8,128)S(1)}, f32[2,128,128]{2,1,0:T(8,128)S(1)}, u32[]{:S(2)}, u32[]{:S(2)}) collective-permute-start(f32[2,128,128]{2,1,0:T(8,128)S(1)} %get-tuple-element.32), channel_id=1, source_target_pairs={{0,32},{16,48},{32,0},{48,16},{1,33},{17,49},{33,1},{49,17},{2,34}... | collective-permute-start | bytes 393224 | tf_op jit(solution)/shard_map/ppermute | solution.py:35
  84.2 1.4 %collective-permute-start.17 = (f32[2,128,128]{2,1,0:T(8,128)S(1)}, f32[2,128,128]{2,1,0:T(8,128)S(1)}, u32[]{:S(2)}, u32[]{:S(2)}) collective-permute-start(f32[2,128,128]{2,1,0:T(8,128)S(1)} %get-tuple-element.29), channel_id=1, source_target_pairs={{0,48},{16,0},{32,16},{48,32},{1,49},{17,1},{33,17},{49,33},{2,50}... | collective-permute-start | bytes 393224 | tf_op jit(solution)/shard_map/ppermute | solution.py:35
  85.7 4.7 %collective-permute-done.26 = f32[512,128]{1,0:T(8,128)S(1)} collective-permute-done((f32[512,128]{1,0:T(8,128)S(1)}, f32[512,128]{1,0:T(8,128)S(1)}, u32[]{:S(2)}, u32[]{:S(2)}) %collective-permute-start.26) | collective-permute-done | bytes 262176 | tf_op jit(solution)/shard_map/ppermute | solution.py:35
  90.4 0.7 fusion.22
  91.1 3.6 %collective-permute-start.28 = (f32[2,128,128]{2,1,0:T(8,128)S(1)}, f32[2,128,128]{2,1,0:T(8,128)S(1)}, u32[]{:S(2)}, u32[]{:S(2)}) collective-permute-start(f32[2,128,128]{2,1,0:T(8,128)S(1)} %get-tuple-element.28), channel_id=1, source_target_pairs={{0,32},{16,48},{32,0},{48,16},{1,33},{17,49},{33,1},{49,17},{2,34}... | collective-permute-start | bytes 393224 | tf_op jit(solution)/shard_map/ppermute | solution.py:35
  94.7 0.7 stack.107.order
  95.4 0.7 collective-permute-done.27.refs_5_
  96.1 2.6 %collective-permute-done.28.refs_6_ = f32[2,128,128]{2,1,0:T(8,128)S(1)} collective-permute-done((f32[2,128,128]{2,1,0:T(8,128)S(1)}, f32[2,128,128]{2,1,0:T(8,128)S(1)}, u32[]{:S(2)}, u32[]{:S(2)}) %collective-permute-start.28) | collective-permute-done | bytes 131104 | tf_op jit(solution)/shard_map/ppermute | solution.py:35
  98.7 0.3 collective-permute-done.29.refs_7_
  99.0 0.4 copy-done.12
  99.3 0.3 copy-done.13
  99.6 2.4 %shard_map.21 = f32[1,128,2048]{2,1,0:T(8,128)} custom-call(s32[9]{0:T(128)} %stack.107.order, f32[2,128,128]{2,1,0:T(8,128)} %get-tuple-element.30.refs_0_, f32[2,128,128]{2,1,0:T(8,128)} %copy-done.8, f32[2,128,128]{2,1,0:T(8,128)} %copy-done.9, f32[2,128,128]{2,1,0:T(8,128)} %copy-done.10, f32[2,128,128]{2,1,0:T(8,128)} %get-tuple-element.26.refs_4_, ...), custom_call_target="tpu_custom_call" | custom-call | tf_op jit(solution)/shard_map/pallas_call | solution.py:126
  (60 shorter events, 0.7 us)
Async XLA Ops:
  0.0 15.5 %collective-permute-start.3 = (bf16[3,128,512]{2,1,0:T(8,128)(2,1)}, bf16[3,128,512]{2,1,0:T(8,128)(2,1)S(1)}, u32[]{:S(2)}, u32[]{:S(2)}) collective-permute-start(bf16[3,128,512]{2,1,0:T(8,128)(2,1)} %bitcast.66), channel_id=1, source_target_pairs={{0,1},{1,2},{2,3},{3,4},{4,5},{5,6},{6,7},{7,0},{8,9},{9,10},{10,1... | collective-permute-start | bytes 1179656 | tf_op jit(solution)/shard_map/ppermute | solution.py:35
  2.5 13.0 %collective-permute-start.4 = (bf16[3,128,512]{2,1,0:T(8,128)(2,1)}, bf16[3,128,512]{2,1,0:T(8,128)(2,1)S(1)}, u32[]{:S(2)}, u32[]{:S(2)}) collective-permute-start(bf16[3,128,512]{2,1,0:T(8,128)(2,1)} %bitcast.67), channel_id=1, source_target_pairs={{0,7},{1,0},{2,1},{3,2},{4,3},{5,4},{6,5},{7,6},{8,15},{9,8},{10,9... | collective-permute-start | bytes 1179656 | tf_op jit(solution)/shard_map/ppermute | solution.py:35
  6.4 15.8 %collective-permute-start = (bf16[3,128,512]{2,1,0:T(8,128)(2,1)}, bf16[3,128,512]{2,1,0:T(8,128)(2,1)S(1)}, u32[]{:S(2)}, u32[]{:S(2)}) collective-permute-start(bf16[3,128,512]{2,1,0:T(8,128)(2,1)} %bitcast.68), channel_id=1, source_target_pairs={{0,16},{16,32},{32,48},{48,0},{64,112},{80,64},{96,80},{112,96},{1... | collective-permute-start | bytes 1179656 | tf_op jit(solution)/shard_map/ppermute | solution.py:35
  15.5 10.7 %collective-permute-start.5 = (bf16[3,128,512]{2,1,0:T(8,128)(2,1)S(1)}, bf16[3,128,512]{2,1,0:T(8,128)(2,1)}, u32[]{:S(2)}, u32[]{:S(2)}) collective-permute-start(bf16[3,128,512]{2,1,0:T(8,128)(2,1)S(1)} %collective-permute-done.3.refs_5_), channel_id=1, source_target_pairs={{0,1},{1,2},{2,3},{3,4},{4,5},{5,6},{6,7},{7,0},{8,9},{9,10},{10,1... | collective-permute-start | bytes 1179656 | tf_op jit(solution)/shard_map/ppermute | solution.py:35
  15.5 24.2 %copy-start.2 = (bf16[3,128,512]{2,1,0:T(8,128)(2,1)}, bf16[3,128,512]{2,1,0:T(8,128)(2,1)S(1)}, u32[]{:S(2)}) copy-start(bf16[3,128,512]{2,1,0:T(8,128)(2,1)S(1)} %collective-permute-done.4.refs_6_) | copy-start | bytes 1179652
  15.5 10.7 %collective-permute-start.18 = (bf16[3,128,512]{2,1,0:T(8,128)(2,1)S(1)}, bf16[3,128,512]{2,1,0:T(8,128)(2,1)S(1)}, u32[]{:S(2)}, u32[]{:S(2)}) collective-permute-start(bf16[3,128,512]{2,1,0:T(8,128)(2,1)S(1)} %collective-permute-done.4.refs_6_), channel_id=1, source_target_pairs={{0,7},{1,0},{2,1},{3,2},{4,3},{5,4},{6,5},{7,6},{8,15},{9,8},{10,9... | collective-permute-start | bytes 1179656 | tf_op jit(solution)/shard_map/ppermute | solution.py:35
  18.1 10.8 %collective-permute-start.8 = (bf16[3,128,512]{2,1,0:T(8,128)(2,1)}, bf16[3,128,512]{2,1,0:T(8,128)(2,1)S(1)}, u32[]{:S(2)}, u32[]{:S(2)}) collective-permute-start(bf16[3,128,512]{2,1,0:T(8,128)(2,1)} %bitcast.69), channel_id=1, source_target_pairs={{0,8},{8,0},{1,9},{9,1},{2,10},{10,2},{3,11},{11,3},{4,12},{12,4},... | collective-permute-start | bytes 1179656 | tf_op jit(solution)/shard_map/ppermute | solution.py:35
  20.9 10.9 %collective-permute-start.1 = (bf16[3,128,512]{2,1,0:T(8,128)(2,1)}, bf16[3,128,512]{2,1,0:T(8,128)(2,1)S(1)}, u32[]{:S(2)}, u32[]{:S(2)}) collective-permute-start(bf16[3,128,512]{2,1,0:T(8,128)(2,1)} %bitcast.70), channel_id=1, source_target_pairs={{0,48},{16,0},{32,16},{48,32},{64,80},{80,96},{96,112},{112,64},{1... | collective-permute-start | bytes 1179656 | tf_op jit(solution)/shard_map/ppermute | solution.py:35
  22.2 9.6 %collective-permute-start.2 = (bf16[3,128,512]{2,1,0:T(8,128)(2,1)S(1)}, bf16[3,128,512]{2,1,0:T(8,128)(2,1)S(1)}, u32[]{:S(2)}, u32[]{:S(2)}) collective-permute-start(bf16[3,128,512]{2,1,0:T(8,128)(2,1)S(1)} %collective-permute-done.refs_1_), channel_id=1, source_target_pairs={{0,16},{16,32},{32,48},{48,0},{64,112},{80,64},{96,80},{112,96},{1... | collective-permute-start | bytes 1179656 | tf_op jit(solution)/shard_map/ppermute | solution.py:35
  26.2 14.4 %collective-permute-start.19 = (bf16[3,128,512]{2,1,0:T(8,128)(2,1)}, bf16[3,128,512]{2,1,0:T(8,128)(2,1)S(1)}, u32[]{:S(2)}, u32[]{:S(2)}) collective-permute-start(bf16[3,128,512]{2,1,0:T(8,128)(2,1)} %collective-permute-done.5.refs_7_), channel_id=1, source_target_pairs={{0,1},{1,2},{2,3},{3,4},{4,5},{5,6},{6,7},{7,0},{8,9},{9,10},{10,1... | collective-permute-start | bytes 1179656 | tf_op jit(solution)/shard_map/ppermute | solution.py:35
  26.2 17.8 %collective-permute-start.20 = (bf16[3,128,512]{2,1,0:T(8,128)(2,1)S(1)}, bf16[3,128,512]{2,1,0:T(8,128)(2,1)S(1)}, u32[]{:S(2)}, u32[]{:S(2)}) collective-permute-start(bf16[3,128,512]{2,1,0:T(8,128)(2,1)S(1)} %collective-permute-done.18.refs_4_), channel_id=1, source_target_pairs={{0,7},{1,0},{2,1},{3,2},{4,3},{5,4},{6,5},{7,6},{8,15},{9,8},{10,9... | collective-permute-start | bytes 1179656 | tf_op jit(solution)/shard_map/ppermute | solution.py:35
  28.9 15.8 %collective-permute-start.9 = (bf16[3,128,512]{2,1,0:T(8,128)(2,1)S(1)}, bf16[3,128,512]{2,1,0:T(8,128)(2,1)}, u32[]{:S(2)}, u32[]{:S(2)}) collective-permute-start(bf16[3,128,512]{2,1,0:T(8,128)(2,1)S(1)} %collective-permute-done.8.refs_0_), channel_id=1, source_target_pairs={{0,16},{16,32},{32,48},{48,0},{64,112},{80,64},{96,80},{112,96},{1... | collective-permute-start | bytes 1179656 | tf_op jit(solution)/shard_map/ppermute | solution.py:35
  31.8 13.0 %collective-permute-start.10 = (bf16[3,128,512]{2,1,0:T(8,128)(2,1)S(1)}, bf16[3,128,512]{2,1,0:T(8,128)(2,1)}, u32[]{:S(2)}, u32[]{:S(2)}) collective-permute-start(bf16[3,128,512]{2,1,0:T(8,128)(2,1)S(1)} %collective-permute-done.8.refs_0_), channel_id=1, source_target_pairs={{0,48},{16,0},{32,16},{48,32},{64,80},{80,96},{96,112},{112,64},{1... | collective-permute-start | bytes 1179656 | tf_op jit(solution)/shard_map/ppermute | solution.py:35
  31.8 12.9 %collective-permute-start.11 = (bf16[3,128,512]{2,1,0:T(8,128)(2,1)S(1)}, bf16[3,128,512]{2,1,0:T(8,128)(2,1)}, u32[]{:S(2)}, u32[]{:S(2)}) collective-permute-start(bf16[3,128,512]{2,1,0:T(8,128)(2,1)S(1)} %collective-permute-done.2.refs_3_), channel_id=1, source_target_pairs={{0,8},{8,0},{1,9},{9,1},{2,10},{10,2},{3,11},{11,3},{4,12},{12,4},... | collective-permute-start | bytes 1179656 | tf_op jit(solution)/shard_map/ppermute | solution.py:35
  34.6 1.0 copy-start
  39.7 0.8 copy-start.6
  40.5 11.2 %collective-permute-start.6 = (f32[2,512,128]{2,1,0:T(8,128)}, f32[2,512,128]{2,1,0:T(8,128)}, u32[]{:S(2)}, u32[]{:S(2)}) collective-permute-start(f32[2,512,128]{2,1,0:T(8,128)} %get-tuple-element.14), channel_id=1, source_target_pairs={{0,64},{64,0},{1,65},{65,1},{2,66},{66,2},{3,67},{67,3},{4,68},{68... | collective-permute-start | bytes 1572872 | tf_op jit(solution)/shard_map/ppermute | solution.py:35
  43.9 1.1 %copy-start.1 = (bf16[128,3,512]{2,0,1:T(8,128)(2,1)S(1)}, bf16[128,3,512]{2,0,1:T(8,128)(2,1)}, u32[]{:S(2)}) copy-start(bf16[128,3,512]{2,0,1:T(8,128)(2,1)} %param.1) | copy-start | bytes 1179652
  43.9 1.3 %copy-start.3 = (bf16[3,128,512]{2,1,0:T(8,128)(2,1)S(1)}, bf16[3,128,512]{2,1,0:T(8,128)(2,1)}, u32[]{:S(2)}) copy-start(bf16[3,128,512]{2,1,0:T(8,128)(2,1)} %copy-done.2) | copy-start | bytes 1179652
  44.7 8.2 %collective-permute-start.21 = (bf16[3,128,512]{2,1,0:T(8,128)(2,1)}, bf16[3,128,512]{2,1,0:T(8,128)(2,1)}, u32[]{:S(2)}, u32[]{:S(2)}) collective-permute-start(bf16[3,128,512]{2,1,0:T(8,128)(2,1)} %broadcast_select_fusion), channel_id=1, source_target_pairs={{0,1},{1,2},{2,3},{3,4},{4,5},{5,6},{6,7},{7,0},{64,71},{65,64},{6... | collective-permute-start | bytes 1179656 | tf_op jit(solution)/shard_map/ppermute | solution.py:35
  49.7 0.8 copy-start.4
  50.5 10.8 %collective-permute-start.12 = (f32[2,512,128]{2,1,0:T(8,128)}, f32[2,512,128]{2,1,0:T(8,128)}, u32[]{:S(2)}, u32[]{:S(2)}) collective-permute-start(f32[2,512,128]{2,1,0:T(8,128)} %get-tuple-element.16), channel_id=1, source_target_pairs={{0,64},{64,0},{1,65},{65,1},{2,66},{66,2},{3,67},{67,3},{4,68},{68... | collective-permute-start | bytes 1572872 | tf_op jit(solution)/shard_map/ppermute | solution.py:35
  52.7 12.3 %collective-permute-start.7 = (f32[512,128]{1,0:T(8,128)S(1)}, f32[512,128]{1,0:T(8,128)S(1)}, u32[]{:S(2)}, u32[]{:S(2)}) collective-permute-start(f32[512,128]{1,0:T(8,128)S(1)} %fusion.7), channel_id=1, source_target_pairs={{0,128},{128,0},{1,129},{129,1},{2,130},{130,2},{3,131},{131,3},{4... | collective-permute-start | bytes 786440 | tf_op jit(solution)/shard_map/ppermute | solution.py:35
  56.2 5.0 %copy-start.5 = (f32[2,512,128]{2,1,0:T(8,128)S(1)}, f32[2,512,128]{2,1,0:T(8,128)}, u32[]{:S(2)}) copy-start(f32[2,512,128]{2,1,0:T(8,128)} %copy-done.4) | copy-start | bytes 1572868
  56.2 20.6 %collective-permute-start.22 = (f32[2,512,128]{2,1,0:T(8,128)S(1)}, f32[2,512,128]{2,1,0:T(8,128)S(1)}, u32[]{:S(2)}, u32[]{:S(2)}) collective-permute-start(f32[2,512,128]{2,1,0:T(8,128)S(1)} %get-tuple-element.18), channel_id=1, source_target_pairs={{0,64},{64,0},{1,65},{65,1},{2,66},{66,2},{3,67},{67,3},{4,68},{68... | collective-permute-start | bytes 1572872 | tf_op jit(solution)/shard_map/ppermute | solution.py:35
  61.1 15.8 %collective-permute-start.24 = (f32[2,512,128]{2,1,0:T(8,128)S(1)}, f32[2,512,128]{2,1,0:T(8,128)S(1)}, u32[]{:S(2)}, u32[]{:S(2)}) collective-permute-start(f32[2,512,128]{2,1,0:T(8,128)S(1)} %get-tuple-element.20), channel_id=1, source_target_pairs={{0,64},{64,0},{1,65},{65,1},{2,66},{66,2},{3,67},{67,3},{4,68},{68... | collective-permute-start | bytes 1572872 | tf_op jit(solution)/shard_map/ppermute | solution.py:35
  61.3 3.8 %copy-start.7 = (f32[2,512,128]{2,1,0:T(8,128)S(1)}, f32[2,512,128]{2,1,0:T(8,128)}, u32[]{:S(2)}) copy-start(f32[2,512,128]{2,1,0:T(8,128)} %copy-done.6) | copy-start | bytes 1572868
  62.4 14.3 %collective-permute-start.13 = (f32[512,128]{1,0:T(8,128)S(1)}, f32[512,128]{1,0:T(8,128)S(1)}, u32[]{:S(2)}, u32[]{:S(2)}) collective-permute-start(f32[512,128]{1,0:T(8,128)S(1)} %get-tuple-element.24), channel_id=1, source_target_pairs={{0,136},{8,128},{128,8},{136,0},{1,137},{9,129},{129,9},{137,1},{2... | collective-permute-start | bytes 786440 | tf_op jit(solution)/shard_map/ppermute | solution.py:35
  64.2 12.6 %collective-permute-start.14 = (f32[512,128]{1,0:T(8,128)S(1)}, f32[512,128]{1,0:T(8,128)S(1)}, u32[]{:S(2)}, u32[]{:S(2)}) collective-permute-start(f32[512,128]{1,0:T(8,128)S(1)} %get-tuple-element.23), channel_id=1, source_target_pairs={{0,8},{8,0},{1,9},{9,1},{2,10},{10,2},{3,11},{11,3},{4,12},{12,4},... | collective-permute-start | bytes 786440 | tf_op jit(solution)/shard_map/ppermute | solution.py:35
  76.8 7.4 %collective-permute-start.23 = (f32[512,128]{1,0:T(8,128)S(1)}, f32[512,128]{1,0:T(8,128)S(1)}, u32[]{:S(2)}, u32[]{:S(2)}) collective-permute-start(f32[512,128]{1,0:T(8,128)S(1)} %fusion.2), channel_id=1, source_target_pairs={{0,128},{128,0},{1,129},{129,1},{2,130},{130,2},{3,131},{131,3},{4... | collective-permute-start | bytes 786440 | tf_op jit(solution)/shard_map/ppermute | solution.py:35
  77.0 8.7 %collective-permute-start.25 = (f32[512,128]{1,0:T(8,128)S(1)}, f32[512,128]{1,0:T(8,128)S(1)}, u32[]{:S(2)}, u32[]{:S(2)}) collective-permute-start(f32[512,128]{1,0:T(8,128)S(1)} %get-tuple-element.22), channel_id=1, source_target_pairs={{0,136},{8,128},{128,8},{136,0},{1,137},{9,129},{129,9},{137,1},{2... | collective-permute-start | bytes 786440 | tf_op jit(solution)/shard_map/ppermute | solution.py:35
  78.7 11.6 %collective-permute-start.26 = (f32[512,128]{1,0:T(8,128)S(1)}, f32[512,128]{1,0:T(8,128)S(1)}, u32[]{:S(2)}, u32[]{:S(2)}) collective-permute-start(f32[512,128]{1,0:T(8,128)S(1)} %get-tuple-element.21), channel_id=1, source_target_pairs={{0,8},{8,0},{1,9},{9,1},{2,10},{10,2},{3,11},{11,3},{4,12},{12,4},... | collective-permute-start | bytes 786440 | tf_op jit(solution)/shard_map/ppermute | solution.py:35
  81.0 13.7 %collective-permute-start.15 = (f32[2,128,128]{2,1,0:T(8,128)S(1)}, f32[2,128,128]{2,1,0:T(8,128)S(1)}, u32[]{:S(2)}, u32[]{:S(2)}) collective-permute-start(f32[2,128,128]{2,1,0:T(8,128)S(1)} %get-tuple-element.31), channel_id=1, source_target_pairs={{0,16},{16,32},{32,48},{48,0},{1,17},{17,33},{33,49},{49,1},{2,18}... | collective-permute-start | bytes 393224 | tf_op jit(solution)/shard_map/ppermute | solution.py:35
  81.1 14.3 %collective-permute-start.16 = (f32[2,128,128]{2,1,0:T(8,128)S(1)}, f32[2,128,128]{2,1,0:T(8,128)S(1)}, u32[]{:S(2)}, u32[]{:S(2)}) collective-permute-start(f32[2,128,128]{2,1,0:T(8,128)S(1)} %get-tuple-element.32), channel_id=1, source_target_pairs={{0,32},{16,48},{32,0},{48,16},{1,33},{17,49},{33,1},{49,17},{2,34}... | collective-permute-start | bytes 393224 | tf_op jit(solution)/shard_map/ppermute | solution.py:35
  84.2 11.2 %collective-permute-start.17 = (f32[2,128,128]{2,1,0:T(8,128)S(1)}, f32[2,128,128]{2,1,0:T(8,128)S(1)}, u32[]{:S(2)}, u32[]{:S(2)}) collective-permute-start(f32[2,128,128]{2,1,0:T(8,128)S(1)} %get-tuple-element.29), channel_id=1, source_target_pairs={{0,48},{16,0},{32,16},{48,32},{1,49},{17,1},{33,17},{49,33},{2,50}... | collective-permute-start | bytes 393224 | tf_op jit(solution)/shard_map/ppermute | solution.py:35
  91.1 5.0 %collective-permute-start.27 = (f32[2,128,128]{2,1,0:T(8,128)S(1)}, f32[2,128,128]{2,1,0:T(8,128)S(1)}, u32[]{:S(2)}, u32[]{:S(2)}) collective-permute-start(f32[2,128,128]{2,1,0:T(8,128)S(1)} %get-tuple-element.27), channel_id=1, source_target_pairs={{0,16},{16,32},{32,48},{48,0},{1,17},{17,33},{33,49},{49,1},{2,18}... | collective-permute-start | bytes 393224 | tf_op jit(solution)/shard_map/ppermute | solution.py:35
  91.1 7.6 %collective-permute-start.28 = (f32[2,128,128]{2,1,0:T(8,128)S(1)}, f32[2,128,128]{2,1,0:T(8,128)S(1)}, u32[]{:S(2)}, u32[]{:S(2)}) collective-permute-start(f32[2,128,128]{2,1,0:T(8,128)S(1)} %get-tuple-element.28), channel_id=1, source_target_pairs={{0,32},{16,48},{32,0},{48,16},{1,33},{17,49},{33,1},{49,17},{2,34}... | collective-permute-start | bytes 393224 | tf_op jit(solution)/shard_map/ppermute | solution.py:35
  94.7 4.3 %copy-start.8 = (f32[2,128,128]{2,1,0:T(8,128)}, f32[2,128,128]{2,1,0:T(8,128)S(1)}, u32[]{:S(2)}) copy-start(f32[2,128,128]{2,1,0:T(8,128)S(1)} %collective-permute-done.15.refs_1_) | copy-start | bytes 393220
  94.7 4.3 %collective-permute-start.29 = (f32[2,128,128]{2,1,0:T(8,128)S(1)}, f32[2,128,128]{2,1,0:T(8,128)S(1)}, u32[]{:S(2)}, u32[]{:S(2)}) collective-permute-start(f32[2,128,128]{2,1,0:T(8,128)S(1)} %get-tuple-element.25), channel_id=1, source_target_pairs={{0,48},{16,0},{32,16},{48,32},{1,49},{17,1},{33,17},{49,33},{2,50}... | collective-permute-start | bytes 393224 | tf_op jit(solution)/shard_map/ppermute | solution.py:35
  95.4 3.6 %copy-start.9 = (f32[2,128,128]{2,1,0:T(8,128)}, f32[2,128,128]{2,1,0:T(8,128)S(1)}, u32[]{:S(2)}) copy-start(f32[2,128,128]{2,1,0:T(8,128)S(1)} %collective-permute-done.16.refs_2_) | copy-start | bytes 393220
  95.4 3.6 %copy-start.10 = (f32[2,128,128]{2,1,0:T(8,128)}, f32[2,128,128]{2,1,0:T(8,128)S(1)}, u32[]{:S(2)}) copy-start(f32[2,128,128]{2,1,0:T(8,128)S(1)} %collective-permute-done.17.refs_3_) | copy-start | bytes 393220
  96.1 2.8 %copy-start.11 = (f32[2,128,128]{2,1,0:T(8,128)}, f32[2,128,128]{2,1,0:T(8,128)S(1)}, u32[]{:S(2)}) copy-start(f32[2,128,128]{2,1,0:T(8,128)S(1)} %collective-permute-done.27.refs_5_) | copy-start | bytes 393220
  98.7 0.6 copy-start.12
  98.9 0.7 copy-start.13

commit v4 on v2

v4 whole, which is shorter than its diff:
```python
import functools

import jax
import jax.numpy as jnp
from jax import lax
from jax.experimental import pallas as pl
from jax.experimental.pallas import tpu as pltpu
from jax.sharding import Mesh, PartitionSpec as P

XL, CORE, Y, XH, Z = 2, 2, 4, 2, 8
AXES = ("xl", "core", "y", "xh", "z")


def split_mesh(mesh):
    return Mesh(mesh.devices.reshape(XL, CORE, Y, XH, Z), AXES)


def move(value, axes, target):
    sizes = {"xl": XL, "core": CORE, "y": Y, "xh": XH, "z": Z}
    dims = [sizes[a] for a in axes]
    count = 1
    for d in dims:
        count *= d
    pairs = []
    for source in range(count):
        rest, place = source, []
        for d in reversed(dims):
            place.insert(0, rest % d)
            rest //= d
        goal = target(*place)
        flat = 0
        for d, g in zip(dims, goal):
            flat = flat * d + g % d
        pairs.append((source, flat))
    return lax.ppermute(value, axes, pairs)


def turn(core, step):
    return step if core == 0 else -step


def along_z(value, step):
    return move(value, ("core", "z"), lambda c, z: (c, z + turn(c, step)))


def along_y(value, step):
    return move(value, ("core", "y"), lambda c, y: (c, y + turn(c, step)))


def across(value):
    return move(value, ("xh",), lambda h: (h + 1,))


def product_kernel(slots, order, *refs):
    row_blocks, column_blocks = refs[:8], refs[8:16]
    targets = refs[-(len(slots) // 2) - 4 : -4]
    rows, columns, row_sem, column_sem = refs[-4:]
    aux, height, occ = row_blocks[0].shape
    sub = height // 4
    half_slots = len(slots) // 2
    column_copies, row_copies = [[] for _ in range(half_slots)], []
    for n, slot in enumerate(slots):
        for k in range(8):
            first = pl.multiple_of(order[16 + slot] * sub, sub)
            place = pl.multiple_of(n * 8 * sub + order[8 + k] * sub, sub)
            column_copies[n // 2].append(
                pltpu.make_async_copy(
                    column_blocks[k].at[:, pl.ds(first, sub), :],
                    columns.at[:, pl.ds(place, sub), :],
                    column_sem.at[k * len(slots) + n],
                )
            )
    for k in range(8):
        row_copies.append(
            pltpu.make_async_copy(row_blocks[k], rows.at[:, k * height : (k + 1) * height, :], row_sem.at[k])
        )
    for c in column_copies[0] + row_copies:
        c.start()
    for later in column_copies[1:]:
        for c in later:
            c.start()
    for n in range(half_slots):
        for c in column_copies[n]:
            c.wait()
        for t in range(0, 8, 2):
            if n == 0:
                for k in range(t, t + 2):
                    row_copies[k].wait()
            total = None
            for a in range(aux):
                part = lax.dot_general(
                    rows[a, t * height : (t + 2) * height],
                    columns[a, n * 16 * sub : (n + 1) * 16 * sub],
                    (((1,), (1,)), ((), ())),
                    preferred_element_type=jnp.float32,
                )
                total = part if total is None else total + part
            for k in range(t, t + 2):
                place = pl.multiple_of(order[k] * height, height)
                for side in range(2):
                    targets[n][side, pl.ds(place, height), :] = total[
                        (k - t) * height : (k - t + 1) * height, side * 8 * sub : (side + 1) * 8 * sub
                    ]


def products(order, row_blocks, column_blocks, slots, after=()):
    aux, height, occ = row_blocks[0].shape
    shape = jax.ShapeDtypeStruct((2, 8 * height, 2 * height), jnp.float32)
    return pl.pallas_call(
        functools.partial(product_kernel, slots),
        out_shape=[shape] * (len(slots) // 2),
        in_specs=[pl.BlockSpec(memory_space=pltpu.SMEM)] + [pl.BlockSpec(memory_space=pl.ANY)] * (16 + len(after)),
        out_specs=[pl.BlockSpec(memory_space=pltpu.VMEM)] * (len(slots) // 2),
        scratch_shapes=[
            pltpu.VMEM((aux, 8 * height, occ), jnp.bfloat16),
            pltpu.VMEM((aux, len(slots) * 2 * height, occ), jnp.bfloat16),
            pltpu.SemaphoreType.DMA((8,)),
            pltpu.SemaphoreType.DMA((8 * len(slots),)),
        ],
        compiler_params=pltpu.CompilerParams(vmem_limit_bytes=40 * 1024 * 1024),
    )(order, *row_blocks, *column_blocks, *after)


def assemble_kernel(got, out):
    step, height, width = got.shape[1:]
    for p in range(step):
        out[0, :, p * width : (p + 1) * width] = got[0, p] + got[1, p]


def assemble(got):
    count, height, width = got.shape[1:]
    step = 4
    return pl.pallas_call(
        assemble_kernel,
        grid=(count // step,),
        out_shape=jax.ShapeDtypeStruct((1, height, count * width), jnp.float32),
        in_specs=[pl.BlockSpec((2, step, height, width), lambda i: (0, i, 0, 0))],
        out_specs=pl.BlockSpec((1, height, step * width), lambda i: (0, 0, i)),
    )(got)


def per_device(factors):
    own = jnp.transpose(factors, (1, 0, 2))
    core, y, xh, z = (lax.axis_index(a) for a in AXES[1:])
    sign = 1 - 2 * core

    za1 = along_z(own, 1)
    zb1 = along_z(own, -1)
    ya1 = along_y(own, 1)
    yb1 = along_y(own, -1)
    x0 = across(own)
    za2 = along_z(za1, 1)
    zb2 = along_z(zb1, -1)
    ya2 = along_y(ya1, 1)
    xa1 = along_y(x0, 1)
    xb1 = along_y(x0, -1)
    za3 = along_z(za2, 1)
    zb3 = along_z(zb2, -1)
    xa2 = across(ya2)
    za4 = along_z(za3, 1)

    row_blocks = [own, ya1, yb1, ya2, x0, xa1, xb1, xa2]
    dy = [0, -sign, sign, 2]
    row_order = [lax.rem(y + d + 4, 4) * 2 + lax.rem(xh + dx, 2) for dx in range(2) for d in dy]
    column_blocks = [own, za1, zb1, za2, zb2, za3, zb3, za4]
    dz = [0, -sign, sign, -2 * sign, 2 * sign, -3 * sign, 3 * sign, 4]
    column_order = [lax.rem(z + d + 8, 8) for d in dz]
    fit_order = [1 - core, 3 - core, core, 2 + core]
    order = jnp.stack([jnp.int32(v) for v in row_order + column_order + fit_order])
    send, keep = products(order, row_blocks, column_blocks, (0, 1, 2, 3))
    summed = keep + move(send, ("core",), lambda c: (c + 1,))

    height, width = summed.shape[1] // 8, summed.shape[2]
    parts = summed.reshape(2 * 8, height, width)
    got = lax.all_to_all(parts, ("xl", "y", "xh"), split_axis=0, concat_axis=0, tiled=True)
    return assemble(got.reshape(2, 8, height, width))


def solution(mesh):
    return jax.shard_map(
        per_device,
        mesh=split_mesh(mesh),
        in_specs=(P(("y", "xh", "z"), ("xl", "core"), None),),
        out_specs=P(("xl", "core"), ("y", "xh", "z"), None),
        check_vma=False,
    )
```

time: 117 us -> 95.7 us (0.82)
  waiting for transfers between devices: 54.5 us -> 20.4 us
  blocking collectives: 0 us -> 34 us
  starting transfers between devices: 39.8 us -> 30.6 us
  Pallas kernels: 17.8 us -> 9.06 us
  local copies, waits for them, and re-layouts: 2.63 us -> 1.09 us
    ppermute x21 -> x15, waiting for transfers between devices: 54.5 us -> 20.4 us  [move(): return lax.ppermute(value, axes, pairs)]
    all_to_all x0 -> x1, blocking collectives: none -> 34 us  [per_device(): lax.all_to_all(parts, ('xl', 'y', 'xh'), split_axis=0, concat_axis=0, til...]
    ppermute x21 -> x15, starting transfers between devices: 39.8 us -> 30.6 us  [move(): return lax.ppermute(value, axes, pairs)]
    pallas_call x2, Pallas kernels: 17.8 us -> 9.06 us  [the longest x1 6.67 us: products(): pl.pallas_call(functools.partial(product_kernel, slots), out_shape=[shape...]
  transfers between devices with their start and end apart: 21 -> 15, of which waited for: 11 -> 5; matrix products, arithmetic and copies ran while one was open for 1% -> 0% of each run, Pallas kernels for 0% -> 0%
where the time goes in v4:
time: 95.7 us; the launch traced here: 95.5 us
  blocking collectives  34 us (36%)
  starting transfers between devices  30.6 us (32%)
  waiting for transfers between devices  20.4 us (21%)
  Pallas kernels  9.06 us (9%)
  local copies, waits for them, and re-layouts  1.09 us (1%)
    all_to_all x1, blocking collectives, per_device(): lax.all_to_all(parts, ('xl', 'y', 'xh'), split_axis=0, concat_axis=0, til...  34 us
    ppermute x15, starting transfers between devices, move(): return lax.ppermute(value, axes, pairs)  30.6 us
    ppermute x15, waiting for transfers between devices, move(): return lax.ppermute(value, axes, pairs)  20.4 us
    pallas_call x1, Pallas kernels, products(): pl.pallas_call(functools.partial(product_kernel, slots), out_shape=[shape...  6.67 us
    pallas_call x1, Pallas kernels, assemble(): pl.pallas_call(assemble_kernel, grid=(count // step,), out_shape=jax.Shap...  2.39 us
  transfers between devices with their start and end apart: 15, of which 5 were waited for; matrix products, arithmetic and copies ran while one was open for 0% of the time, Pallas kernels for 0%

profile of v4, /device:TPU:1, one launch (start us, length us, event | category | flops | bytes accessed | tf_op | source)
XLA Modules:
  0.0 95.5 jit_solution(17912500374399606568)
XLA Ops:
  0.0 6.4 %collective-permute-start.7 = (bf16[3,128,512]{2,1,0:T(8,128)(2,1)}, bf16[3,128,512]{2,1,0:T(8,128)(2,1)S(1)}, u32[]{:S(2)}, u32[]{:S(2)}) collective-permute-start(bf16[3,128,512]{2,1,0:T(8,128)(2,1)} %bitcast.23), channel_id=1, source_target_pairs={{0,1},{1,2},{2,3},{3,4},{4,5},{5,6},{6,7},{7,0},{64,71},{65,64},{6... | collective-permute-start | bytes 1179656 | tf_op jit(solution)/shard_map/ppermute | solution.py:35
  6.4 0.0 collective-permute-start.8
  6.4 2.7 %collective-permute-start = (bf16[3,128,512]{2,1,0:T(8,128)(2,1)}, bf16[3,128,512]{2,1,0:T(8,128)(2,1)S(1)}, u32[]{:S(2)}, u32[]{:S(2)}) collective-permute-start(bf16[3,128,512]{2,1,0:T(8,128)(2,1)} %bitcast.25), channel_id=1, source_target_pairs={{0,16},{16,32},{32,48},{48,0},{64,112},{80,64},{96,80},{112,96},{1... | collective-permute-start | bytes 1179656 | tf_op jit(solution)/shard_map/ppermute | solution.py:35
  9.1 5.4 %collective-permute-done.7.refs_9_ = bf16[3,128,512]{2,1,0:T(8,128)(2,1)S(1)} collective-permute-done((bf16[3,128,512]{2,1,0:T(8,128)(2,1)}, bf16[3,128,512]{2,1,0:T(8,128)(2,1)S(1)}, u32[]{:S(2)}, u32[]{:S(2)}) %collective-permute-start.7) | collective-permute-done | bytes 393248 | tf_op jit(solution)/shard_map/ppermute | solution.py:35
  14.5 3.3 %collective-permute-start.9 = (bf16[3,128,512]{2,1,0:T(8,128)(2,1)S(1)}, bf16[3,128,512]{2,1,0:T(8,128)(2,1)S(1)}, u32[]{:S(2)}, u32[]{:S(2)}) collective-permute-start(bf16[3,128,512]{2,1,0:T(8,128)(2,1)S(1)} %collective-permute-done.7.refs_9_), channel_id=1, source_target_pairs={{0,1},{1,2},{2,3},{3,4},{4,5},{5,6},{6,7},{7,0},{64,71},{65,64},{6... | collective-permute-start | bytes 1179656 | tf_op jit(solution)/shard_map/ppermute | solution.py:35
  17.8 2.7 %collective-permute-start.3 = (bf16[3,128,512]{2,1,0:T(8,128)(2,1)}, bf16[3,128,512]{2,1,0:T(8,128)(2,1)S(1)}, u32[]{:S(2)}, u32[]{:S(2)}) collective-permute-start(bf16[3,128,512]{2,1,0:T(8,128)(2,1)} %bitcast.26), channel_id=1, source_target_pairs={{0,8},{8,0},{1,9},{9,1},{2,10},{10,2},{3,11},{11,3},{4,12},{12,4},... | collective-permute-start | bytes 1179656 | tf_op jit(solution)/shard_map/ppermute | solution.py:35
  20.6 1.3 %collective-permute-start.1 = (bf16[3,128,512]{2,1,0:T(8,128)(2,1)}, bf16[3,128,512]{2,1,0:T(8,128)(2,1)S(1)}, u32[]{:S(2)}, u32[]{:S(2)}) collective-permute-start(bf16[3,128,512]{2,1,0:T(8,128)(2,1)} %bitcast.27), channel_id=1, source_target_pairs={{0,48},{16,0},{32,16},{48,32},{64,80},{80,96},{96,112},{112,64},{1... | collective-permute-start | bytes 1179656 | tf_op jit(solution)/shard_map/ppermute | solution.py:35
  21.8 0.0 collective-permute-done.8.refs_10_
  21.9 0.0 collective-permute-start.10
  21.9 0.0 collective-permute-done.refs_1_
  21.9 1.5 %collective-permute-start.2 = (bf16[3,128,512]{2,1,0:T(8,128)(2,1)S(1)}, bf16[3,128,512]{2,1,0:T(8,128)(2,1)S(1)}, u32[]{:S(2)}, u32[]{:S(2)}) collective-permute-start(bf16[3,128,512]{2,1,0:T(8,128)(2,1)S(1)} %collective-permute-done.refs_1_), channel_id=1, source_target_pairs={{0,16},{16,32},{32,48},{48,0},{64,112},{80,64},{96,80},{112,96},{1... | collective-permute-start | bytes 1179656 | tf_op jit(solution)/shard_map/ppermute | solution.py:35
  23.4 0.0 collective-permute-done.9.refs_11_
  23.4 2.6 %collective-permute-start.11 = (bf16[3,128,512]{2,1,0:T(8,128)(2,1)S(1)}, bf16[3,128,512]{2,1,0:T(8,128)(2,1)S(1)}, u32[]{:S(2)}, u32[]{:S(2)}) collective-permute-start(bf16[3,128,512]{2,1,0:T(8,128)(2,1)S(1)} %collective-permute-done.9.refs_11_), channel_id=1, source_target_pairs={{0,1},{1,2},{2,3},{3,4},{4,5},{5,6},{6,7},{7,0},{64,71},{65,64},{6... | collective-permute-start | bytes 1179656 | tf_op jit(solution)/shard_map/ppermute | solution.py:35
  26.0 2.7 %collective-permute-done.3.refs_4_ = bf16[3,128,512]{2,1,0:T(8,128)(2,1)S(1)} collective-permute-done((bf16[3,128,512]{2,1,0:T(8,128)(2,1)}, bf16[3,128,512]{2,1,0:T(8,128)(2,1)S(1)}, u32[]{:S(2)}, u32[]{:S(2)}) %collective-permute-start.3) | collective-permute-done | bytes 393248 | tf_op jit(solution)/shard_map/ppermute | solution.py:35
  28.7 1.3 %collective-permute-start.5 = (bf16[3,128,512]{2,1,0:T(8,128)(2,1)S(1)}, bf16[3,128,512]{2,1,0:T(8,128)(2,1)}, u32[]{:S(2)}, u32[]{:S(2)}) collective-permute-start(bf16[3,128,512]{2,1,0:T(8,128)(2,1)S(1)} %collective-permute-done.3.refs_4_), channel_id=1, source_target_pairs={{0,48},{16,0},{32,16},{48,32},{64,80},{80,96},{96,112},{112,64},{1... | collective-permute-start | bytes 1179656 | tf_op jit(solution)/shard_map/ppermute | solution.py:35
  30.0 0.0 collective-permute-done.1.refs_2_
  30.0 2.0 %collective-permute-start.4 = (bf16[3,128,512]{2,1,0:T(8,128)(2,1)S(1)}, bf16[3,128,512]{2,1,0:T(8,128)(2,1)}, u32[]{:S(2)}, u32[]{:S(2)}) collective-permute-start(bf16[3,128,512]{2,1,0:T(8,128)(2,1)S(1)} %collective-permute-done.3.refs_4_), channel_id=1, source_target_pairs={{0,16},{16,32},{32,48},{48,0},{64,112},{80,64},{96,80},{112,96},{1... | collective-permute-start | bytes 1179656 | tf_op jit(solution)/shard_map/ppermute | solution.py:35
  31.9 0.0 collective-permute-done.10.refs_12_
  31.9 0.0 collective-permute-start.12
  31.9 0.0 collective-permute-done.2.refs_3_
  31.9 2.6 %collective-permute-start.6 = (bf16[3,128,512]{2,1,0:T(8,128)(2,1)S(1)}, bf16[3,128,512]{2,1,0:T(8,128)(2,1)}, u32[]{:S(2)}, u32[]{:S(2)}) collective-permute-start(bf16[3,128,512]{2,1,0:T(8,128)(2,1)S(1)} %collective-permute-done.2.refs_3_), channel_id=1, source_target_pairs={{0,8},{8,0},{1,9},{9,1},{2,10},{10,2},{3,11},{11,3},{4,12},{12,4},... | collective-permute-start | bytes 1179656 | tf_op jit(solution)/shard_map/ppermute | solution.py:35
  34.5 0.0 collective-permute-done.11.refs_13_
  34.5 3.2 %collective-permute-start.13 = (bf16[3,128,512]{2,1,0:T(8,128)(2,1)S(1)}, bf16[3,128,512]{2,1,0:T(8,128)(2,1)}, u32[]{:S(2)}, u32[]{:S(2)}) collective-permute-start(bf16[3,128,512]{2,1,0:T(8,128)(2,1)S(1)} %collective-permute-done.11.refs_13_), channel_id=1, source_target_pairs={{0,1},{1,2},{2,3},{3,4},{4,5},{5,6},{6,7},{7,0},{64,71},{65,64},{6... | collective-permute-start | bytes 1179656 | tf_op jit(solution)/shard_map/ppermute | solution.py:35
  37.7 0.1 stack.83.order
  37.8 3.2 %collective-permute-done.5.refs_6_ = bf16[3,128,512]{2,1,0:T(8,128)(2,1)} collective-permute-done((bf16[3,128,512]{2,1,0:T(8,128)(2,1)S(1)}, bf16[3,128,512]{2,1,0:T(8,128)(2,1)}, u32[]{:S(2)}, u32[]{:S(2)}) %collective-permute-start.5) | collective-permute-done | bytes 393248 | tf_op jit(solution)/shard_map/ppermute | solution.py:35
  41.1 0.0 collective-permute-done.4.refs_5_
  41.1 0.0 collective-permute-done.12.refs_14_
  41.1 0.0 collective-permute-done.6.refs_7_
  41.1 5.3 %collective-permute-done.13.refs_15_ = bf16[3,128,512]{2,1,0:T(8,128)(2,1)} collective-permute-done((bf16[3,128,512]{2,1,0:T(8,128)(2,1)S(1)}, bf16[3,128,512]{2,1,0:T(8,128)(2,1)}, u32[]{:S(2)}, u32[]{:S(2)}) %collective-permute-start.13) | collective-permute-done | bytes 393248 | tf_op jit(solution)/shard_map/ppermute | solution.py:35
  46.3 0.0 copy-start
  46.3 1.0 %copy-done = bf16[128,3,512]{2,0,1:T(8,128)(2,1)S(1)} copy-done((bf16[128,3,512]{2,0,1:T(8,128)(2,1)S(1)}, bf16[128,3,512]{2,0,1:T(8,128)(2,1)}, u32[]{:S(2)}) %copy-start) | copy-done | bytes 393240
  47.3 6.7 %shard_map.17 = (f32[2,1024,256]{2,1,0:T(8,128)S(1)}, f32[2,1024,256]{2,1,0:T(8,128)S(1)}) custom-call(s32[20]{0:T(128)S(1)} %stack.83.order, bf16[3,128,512]{2,1,0:T(8,128)(2,1)S(1)} %bitcast.28, bf16[3,128,512]{2,1,0:T(8,128)(2,1)S(1)} %collective-permute-done.refs_1_, bf16[3,128,512]{2,1,0:T(8,128)(2,1)S(1)} %collective-permute-done.1.refs_2_, ...), custom_call_target="tpu_custom_call" | custom-call | tf_op jit(solution)/shard_map/pallas_call | solution.py:109
  54.0 1.0 %collective-permute-start.14 = (f32[2,1024,256]{2,1,0:T(8,128)S(1)}, f32[2,1024,256]{2,1,0:T(8,128)S(1)}, u32[]{:S(2)}, u32[]{:S(2)}) collective-permute-start(f32[2,1024,256]{2,1,0:T(8,128)S(1)} %get-tuple-element.8), channel_id=1, source_target_pairs={{0,64},{64,0},{1,65},{65,1},{2,66},{66,2},{3,67},{67,3},{4,68},{68... | collective-permute-start | bytes 6291464 | tf_op jit(solution)/shard_map/ppermute | solution.py:35
  55.0 3.8 %collective-permute-done.14 = f32[2,1024,256]{2,1,0:T(8,128)S(1)} collective-permute-done((f32[2,1024,256]{2,1,0:T(8,128)S(1)}, f32[2,1024,256]{2,1,0:T(8,128)S(1)}, u32[]{:S(2)}, u32[]{:S(2)}) %collective-permute-start.14) | collective-permute-done | bytes 2097184 | tf_op jit(solution)/shard_map/ppermute | solution.py:35
  58.8 0.3 add.139
  59.1 34.0 %all_to_all.5 = f32[16,128,256]{2,1,0:T(8,128)} all-to-all(f32[16,128,256]{2,1,0:T(8,128)S(1)} %bitcast.30), channel_id=1, replica_groups=mesh['xl'=2,'core'=2,'y'=4,'xh'=2,'z'=8] {'xl','y','xh'}, dimensions={0} | all-to-all | bytes 4194304 | tf_op jit(solution)/shard_map/all_to_all | solution.py:175
  93.1 2.4 %shard_map.18 = f32[1,128,2048]{2,1,0:T(8,128)} custom-call(f32[2,8,128,256]{3,2,1,0:T(8,128)} %bitcast.31), custom_call_target="tpu_custom_call" | custom-call | tf_op jit(solution)/shard_map/pallas_call | solution.py:133
Async XLA Ops:
  0.0 14.5 %collective-permute-start.7 = (bf16[3,128,512]{2,1,0:T(8,128)(2,1)}, bf16[3,128,512]{2,1,0:T(8,128)(2,1)S(1)}, u32[]{:S(2)}, u32[]{:S(2)}) collective-permute-start(bf16[3,128,512]{2,1,0:T(8,128)(2,1)} %bitcast.23), channel_id=1, source_target_pairs={{0,1},{1,2},{2,3},{3,4},{4,5},{5,6},{6,7},{7,0},{64,71},{65,64},{6... | collective-permute-start | bytes 1179656 | tf_op jit(solution)/shard_map/ppermute | solution.py:35
  6.4 15.4 %collective-permute-start.8 = (bf16[3,128,512]{2,1,0:T(8,128)(2,1)}, bf16[3,128,512]{2,1,0:T(8,128)(2,1)S(1)}, u32[]{:S(2)}, u32[]{:S(2)}) collective-permute-start(bf16[3,128,512]{2,1,0:T(8,128)(2,1)} %bitcast.24), channel_id=1, source_target_pairs={{0,7},{1,0},{2,1},{3,2},{4,3},{5,4},{6,5},{7,6},{64,65},{65,66},{6... | collective-permute-start | bytes 1179656 | tf_op jit(solution)/shard_map/ppermute | solution.py:35
  6.4 15.4 %collective-permute-start = (bf16[3,128,512]{2,1,0:T(8,128)(2,1)}, bf16[3,128,512]{2,1,0:T(8,128)(2,1)S(1)}, u32[]{:S(2)}, u32[]{:S(2)}) collective-permute-start(bf16[3,128,512]{2,1,0:T(8,128)(2,1)} %bitcast.25), channel_id=1, source_target_pairs={{0,16},{16,32},{32,48},{48,0},{64,112},{80,64},{96,80},{112,96},{1... | collective-permute-start | bytes 1179656 | tf_op jit(solution)/shard_map/ppermute | solution.py:35
  14.5 8.9 %collective-permute-start.9 = (bf16[3,128,512]{2,1,0:T(8,128)(2,1)S(1)}, bf16[3,128,512]{2,1,0:T(8,128)(2,1)S(1)}, u32[]{:S(2)}, u32[]{:S(2)}) collective-permute-start(bf16[3,128,512]{2,1,0:T(8,128)(2,1)S(1)} %collective-permute-done.7.refs_9_), channel_id=1, source_target_pairs={{0,1},{1,2},{2,3},{3,4},{4,5},{5,6},{6,7},{7,0},{64,71},{65,64},{6... | collective-permute-start | bytes 1179656 | tf_op jit(solution)/shard_map/ppermute | solution.py:35
  17.8 10.9 %collective-permute-start.3 = (bf16[3,128,512]{2,1,0:T(8,128)(2,1)}, bf16[3,128,512]{2,1,0:T(8,128)(2,1)S(1)}, u32[]{:S(2)}, u32[]{:S(2)}) collective-permute-start(bf16[3,128,512]{2,1,0:T(8,128)(2,1)} %bitcast.26), channel_id=1, source_target_pairs={{0,8},{8,0},{1,9},{9,1},{2,10},{10,2},{3,11},{11,3},{4,12},{12,4},... | collective-permute-start | bytes 1179656 | tf_op jit(solution)/shard_map/ppermute | solution.py:35
  20.6 9.4 %collective-permute-start.1 = (bf16[3,128,512]{2,1,0:T(8,128)(2,1)}, bf16[3,128,512]{2,1,0:T(8,128)(2,1)S(1)}, u32[]{:S(2)}, u32[]{:S(2)}) collective-permute-start(bf16[3,128,512]{2,1,0:T(8,128)(2,1)} %bitcast.27), channel_id=1, source_target_pairs={{0,48},{16,0},{32,16},{48,32},{64,80},{80,96},{96,112},{112,64},{1... | collective-permute-start | bytes 1179656 | tf_op jit(solution)/shard_map/ppermute | solution.py:35
  21.9 10.1 %collective-permute-start.10 = (bf16[3,128,512]{2,1,0:T(8,128)(2,1)S(1)}, bf16[3,128,512]{2,1,0:T(8,128)(2,1)S(1)}, u32[]{:S(2)}, u32[]{:S(2)}) collective-permute-start(bf16[3,128,512]{2,1,0:T(8,128)(2,1)S(1)} %collective-permute-done.8.refs_10_), channel_id=1, source_target_pairs={{0,7},{1,0},{2,1},{3,2},{4,3},{5,4},{6,5},{7,6},{64,65},{65,66},{6... | collective-permute-start | bytes 1179656 | tf_op jit(solution)/shard_map/ppermute | solution.py:35
  21.9 10.1 %collective-permute-start.2 = (bf16[3,128,512]{2,1,0:T(8,128)(2,1)S(1)}, bf16[3,128,512]{2,1,0:T(8,128)(2,1)S(1)}, u32[]{:S(2)}, u32[]{:S(2)}) collective-permute-start(bf16[3,128,512]{2,1,0:T(8,128)(2,1)S(1)} %collective-permute-done.refs_1_), channel_id=1, source_target_pairs={{0,16},{16,32},{32,48},{48,0},{64,112},{80,64},{96,80},{112,96},{1... | collective-permute-start | bytes 1179656 | tf_op jit(solution)/shard_map/ppermute | solution.py:35
  23.4 11.1 %collective-permute-start.11 = (bf16[3,128,512]{2,1,0:T(8,128)(2,1)S(1)}, bf16[3,128,512]{2,1,0:T(8,128)(2,1)S(1)}, u32[]{:S(2)}, u32[]{:S(2)}) collective-permute-start(bf16[3,128,512]{2,1,0:T(8,128)(2,1)S(1)} %collective-permute-done.9.refs_11_), channel_id=1, source_target_pairs={{0,1},{1,2},{2,3},{3,4},{4,5},{5,6},{6,7},{7,0},{64,71},{65,64},{6... | collective-permute-start | bytes 1179656 | tf_op jit(solution)/shard_map/ppermute | solution.py:35
  28.7 12.4 %collective-permute-start.5 = (bf16[3,128,512]{2,1,0:T(8,128)(2,1)S(1)}, bf16[3,128,512]{2,1,0:T(8,128)(2,1)}, u32[]{:S(2)}, u32[]{:S(2)}) collective-permute-start(bf16[3,128,512]{2,1,0:T(8,128)(2,1)S(1)} %collective-permute-done.3.refs_4_), channel_id=1, source_target_pairs={{0,48},{16,0},{32,16},{48,32},{64,80},{80,96},{96,112},{112,64},{1... | collective-permute-start | bytes 1179656 | tf_op jit(solution)/shard_map/ppermute | solution.py:35
  30.0 11.1 %collective-permute-start.4 = (bf16[3,128,512]{2,1,0:T(8,128)(2,1)S(1)}, bf16[3,128,512]{2,1,0:T(8,128)(2,1)}, u32[]{:S(2)}, u32[]{:S(2)}) collective-permute-start(bf16[3,128,512]{2,1,0:T(8,128)(2,1)S(1)} %collective-permute-done.3.refs_4_), channel_id=1, source_target_pairs={{0,16},{16,32},{32,48},{48,0},{64,112},{80,64},{96,80},{112,96},{1... | collective-permute-start | bytes 1179656 | tf_op jit(solution)/shard_map/ppermute | solution.py:35
  31.9 9.1 %collective-permute-start.12 = (bf16[3,128,512]{2,1,0:T(8,128)(2,1)S(1)}, bf16[3,128,512]{2,1,0:T(8,128)(2,1)}, u32[]{:S(2)}, u32[]{:S(2)}) collective-permute-start(bf16[3,128,512]{2,1,0:T(8,128)(2,1)S(1)} %collective-permute-done.10.refs_12_), channel_id=1, source_target_pairs={{0,7},{1,0},{2,1},{3,2},{4,3},{5,4},{6,5},{7,6},{64,65},{65,66},{6... | collective-permute-start | bytes 1179656 | tf_op jit(solution)/shard_map/ppermute | solution.py:35
  31.9 9.1 %collective-permute-start.6 = (bf16[3,128,512]{2,1,0:T(8,128)(2,1)S(1)}, bf16[3,128,512]{2,1,0:T(8,128)(2,1)}, u32[]{:S(2)}, u32[]{:S(2)}) collective-permute-start(bf16[3,128,512]{2,1,0:T(8,128)(2,1)S(1)} %collective-permute-done.2.refs_3_), channel_id=1, source_target_pairs={{0,8},{8,0},{1,9},{9,1},{2,10},{10,2},{3,11},{11,3},{4,12},{12,4},... | collective-permute-start | bytes 1179656 | tf_op jit(solution)/shard_map/ppermute | solution.py:35
  34.5 11.9 %collective-permute-start.13 = (bf16[3,128,512]{2,1,0:T(8,128)(2,1)S(1)}, bf16[3,128,512]{2,1,0:T(8,128)(2,1)}, u32[]{:S(2)}, u32[]{:S(2)}) collective-permute-start(bf16[3,128,512]{2,1,0:T(8,128)(2,1)S(1)} %collective-permute-done.11.refs_13_), channel_id=1, source_target_pairs={{0,1},{1,2},{2,3},{3,4},{4,5},{5,6},{6,7},{7,0},{64,71},{65,64},{6... | collective-permute-start | bytes 1179656 | tf_op jit(solution)/shard_map/ppermute | solution.py:35
  46.3 1.0 %copy-start = (bf16[128,3,512]{2,0,1:T(8,128)(2,1)S(1)}, bf16[128,3,512]{2,0,1:T(8,128)(2,1)}, u32[]{:S(2)}) copy-start(bf16[128,3,512]{2,0,1:T(8,128)(2,1)} %param.1) | copy-start | bytes 1179652
  54.0 4.8 %collective-permute-start.14 = (f32[2,1024,256]{2,1,0:T(8,128)S(1)}, f32[2,1024,256]{2,1,0:T(8,128)S(1)}, u32[]{:S(2)}, u32[]{:S(2)}) collective-permute-start(f32[2,1024,256]{2,1,0:T(8,128)S(1)} %get-tuple-element.8), channel_id=1, source_target_pairs={{0,64},{64,0},{1,65},{65,1},{2,66},{66,2},{3,67},{67,3},{4,68},{68... | collective-permute-start | bytes 6291464 | tf_op jit(solution)/shard_map/ppermute | solution.py:35

commit v5 on v4

--- a/solution.py
+++ b/solution.py
@@ -117,7 +117,7 @@
             pltpu.SemaphoreType.DMA((8,)),
             pltpu.SemaphoreType.DMA((8 * len(slots),)),
         ],
-        compiler_params=pltpu.CompilerParams(vmem_limit_bytes=40 * 1024 * 1024),
+        compiler_params=pltpu.CompilerParams(vmem_limit_bytes=16 * 1024 * 1024),
     )(order, *row_blocks, *column_blocks, *after)
 
 
@@ -167,7 +167,8 @@
     column_order = [lax.rem(z + d + 8, 8) for d in dz]
     fit_order = [1 - core, 3 - core, core, 2 + core]
     order = jnp.stack([jnp.int32(v) for v in row_order + column_order + fit_order])
-    send, keep = products(order, row_blocks, column_blocks, (0, 1, 2, 3))
+    (send,) = products(order, row_blocks, column_blocks, (0, 1))
+    (keep,) = products(order, row_blocks, column_blocks, (2, 3), (send,))
     summed = keep + move(send, ("core",), lambda c: (c + 1,))
 
     height, width = summed.shape[1] // 8, summed.shape[2]

time: 95.7 us -> 95.4 us (level)
  waiting for transfers between devices: 20.4 us -> 16.6 us
  Pallas kernels: 9.06 us -> 11.8 us
    ppermute x15, waiting for transfers between devices: 20.4 us -> 16.6 us  [move(): return lax.ppermute(value, axes, pairs)]
    pallas_call x1 -> x2, Pallas kernels: 6.67 us -> 9.39 us  [products(): pl.pallas_call(functools.partial(product_kernel, slots), out_shape=[shape...]
  transfers between devices with their start and end apart: 15 -> 15, of which waited for: 5 -> 4; matrix products, arithmetic and copies ran while one was open for 0% -> 0% of each run, Pallas kernels for 0% -> 5%
where the time goes in v5:
time: 95.4 us; the launch traced here: 95.2 us
  blocking collectives  34.6 us (36%)
  starting transfers between devices  30.8 us (32%)
  waiting for transfers between devices  16.6 us (17%)
  Pallas kernels  11.8 us (12%)
  local copies, waits for them, and re-layouts  1.09 us (1%)
    all_to_all x1, blocking collectives, per_device(): lax.all_to_all(parts, ('xl', 'y', 'xh'), split_axis=0, concat_axis=0, til...  34.6 us
    ppermute x15, starting transfers between devices, move(): return lax.ppermute(value, axes, pairs)  30.8 us
    ppermute x15, waiting for transfers between devices, move(): return lax.ppermute(value, axes, pairs)  16.6 us
    pallas_call x2, Pallas kernels, products(): pl.pallas_call(functools.partial(product_kernel, slots), out_shape=[shape...  9.39 us
    pallas_call x1, Pallas kernels, assemble(): pl.pallas_call(assemble_kernel, grid=(count // step,), out_shape=jax.Shap...  2.39 us
  transfers between devices with their start and end apart: 15, of which 4 were waited for; matrix products, arithmetic and copies ran while one was open for 0% of the time, Pallas kernels for 5%

profile of v5, /device:TPU:1, one launch (start us, length us, event | category | flops | bytes accessed | tf_op | source)
XLA Modules:
  0.0 95.2 jit_solution(1696229520389197937)
XLA Ops:
  0.0 6.4 %collective-permute-start.7 = (bf16[3,128,512]{2,1,0:T(8,128)(2,1)}, bf16[3,128,512]{2,1,0:T(8,128)(2,1)S(1)}, u32[]{:S(2)}, u32[]{:S(2)}) collective-permute-start(bf16[3,128,512]{2,1,0:T(8,128)(2,1)} %bitcast.23), channel_id=1, source_target_pairs={{0,1},{1,2},{2,3},{3,4},{4,5},{5,6},{6,7},{7,0},{64,71},{65,64},{6... | collective-permute-start | bytes 1179656 | tf_op jit(solution)/shard_map/ppermute | solution.py:35
  6.4 0.0 collective-permute-start.8
  6.4 2.7 %collective-permute-start = (bf16[3,128,512]{2,1,0:T(8,128)(2,1)}, bf16[3,128,512]{2,1,0:T(8,128)(2,1)S(1)}, u32[]{:S(2)}, u32[]{:S(2)}) collective-permute-start(bf16[3,128,512]{2,1,0:T(8,128)(2,1)} %bitcast.25), channel_id=1, source_target_pairs={{0,16},{16,32},{32,48},{48,0},{64,112},{80,64},{96,80},{112,96},{1... | collective-permute-start | bytes 1179656 | tf_op jit(solution)/shard_map/ppermute | solution.py:35
  9.1 5.4 %collective-permute-done.7.refs_9_ = bf16[3,128,512]{2,1,0:T(8,128)(2,1)S(1)} collective-permute-done((bf16[3,128,512]{2,1,0:T(8,128)(2,1)}, bf16[3,128,512]{2,1,0:T(8,128)(2,1)S(1)}, u32[]{:S(2)}, u32[]{:S(2)}) %collective-permute-start.7) | collective-permute-done | bytes 393248 | tf_op jit(solution)/shard_map/ppermute | solution.py:35
  14.5 3.3 %collective-permute-start.9 = (bf16[3,128,512]{2,1,0:T(8,128)(2,1)S(1)}, bf16[3,128,512]{2,1,0:T(8,128)(2,1)S(1)}, u32[]{:S(2)}, u32[]{:S(2)}) collective-permute-start(bf16[3,128,512]{2,1,0:T(8,128)(2,1)S(1)} %collective-permute-done.7.refs_9_), channel_id=1, source_target_pairs={{0,1},{1,2},{2,3},{3,4},{4,5},{5,6},{6,7},{7,0},{64,71},{65,64},{6... | collective-permute-start | bytes 1179656 | tf_op jit(solution)/shard_map/ppermute | solution.py:35
  17.8 2.7 %collective-permute-start.3 = (bf16[3,128,512]{2,1,0:T(8,128)(2,1)}, bf16[3,128,512]{2,1,0:T(8,128)(2,1)S(1)}, u32[]{:S(2)}, u32[]{:S(2)}) collective-permute-start(bf16[3,128,512]{2,1,0:T(8,128)(2,1)} %bitcast.26), channel_id=1, source_target_pairs={{0,8},{8,0},{1,9},{9,1},{2,10},{10,2},{3,11},{11,3},{4,12},{12,4},... | collective-permute-start | bytes 1179656 | tf_op jit(solution)/shard_map/ppermute | solution.py:35
  20.6 1.3 %collective-permute-start.1 = (bf16[3,128,512]{2,1,0:T(8,128)(2,1)}, bf16[3,128,512]{2,1,0:T(8,128)(2,1)S(1)}, u32[]{:S(2)}, u32[]{:S(2)}) collective-permute-start(bf16[3,128,512]{2,1,0:T(8,128)(2,1)} %bitcast.27), channel_id=1, source_target_pairs={{0,48},{16,0},{32,16},{48,32},{64,80},{80,96},{96,112},{112,64},{1... | collective-permute-start | bytes 1179656 | tf_op jit(solution)/shard_map/ppermute | solution.py:35
  21.8 0.0 collective-permute-done.8.refs_10_
  21.9 0.0 collective-permute-start.10
  21.9 0.0 collective-permute-done.refs_1_
  21.9 1.5 %collective-permute-start.2 = (bf16[3,128,512]{2,1,0:T(8,128)(2,1)S(1)}, bf16[3,128,512]{2,1,0:T(8,128)(2,1)S(1)}, u32[]{:S(2)}, u32[]{:S(2)}) collective-permute-start(bf16[3,128,512]{2,1,0:T(8,128)(2,1)S(1)} %collective-permute-done.refs_1_), channel_id=1, source_target_pairs={{0,16},{16,32},{32,48},{48,0},{64,112},{80,64},{96,80},{112,96},{1... | collective-permute-start | bytes 1179656 | tf_op jit(solution)/shard_map/ppermute | solution.py:35
  23.4 0.0 collective-permute-done.9.refs_11_
  23.4 2.6 %collective-permute-start.11 = (bf16[3,128,512]{2,1,0:T(8,128)(2,1)S(1)}, bf16[3,128,512]{2,1,0:T(8,128)(2,1)S(1)}, u32[]{:S(2)}, u32[]{:S(2)}) collective-permute-start(bf16[3,128,512]{2,1,0:T(8,128)(2,1)S(1)} %collective-permute-done.9.refs_11_), channel_id=1, source_target_pairs={{0,1},{1,2},{2,3},{3,4},{4,5},{5,6},{6,7},{7,0},{64,71},{65,64},{6... | collective-permute-start | bytes 1179656 | tf_op jit(solution)/shard_map/ppermute | solution.py:35
  26.0 2.7 %collective-permute-done.3.refs_4_ = bf16[3,128,512]{2,1,0:T(8,128)(2,1)S(1)} collective-permute-done((bf16[3,128,512]{2,1,0:T(8,128)(2,1)}, bf16[3,128,512]{2,1,0:T(8,128)(2,1)S(1)}, u32[]{:S(2)}, u32[]{:S(2)}) %collective-permute-start.3) | collective-permute-done | bytes 393248 | tf_op jit(solution)/shard_map/ppermute | solution.py:35
  28.7 1.3 %collective-permute-start.5 = (bf16[3,128,512]{2,1,0:T(8,128)(2,1)S(1)}, bf16[3,128,512]{2,1,0:T(8,128)(2,1)}, u32[]{:S(2)}, u32[]{:S(2)}) collective-permute-start(bf16[3,128,512]{2,1,0:T(8,128)(2,1)S(1)} %collective-permute-done.3.refs_4_), channel_id=1, source_target_pairs={{0,48},{16,0},{32,16},{48,32},{64,80},{80,96},{96,112},{112,64},{1... | collective-permute-start | bytes 1179656 | tf_op jit(solution)/shard_map/ppermute | solution.py:35
  30.0 0.0 collective-permute-done.1.refs_2_
  30.0 2.0 %collective-permute-start.4 = (bf16[3,128,512]{2,1,0:T(8,128)(2,1)S(1)}, bf16[3,128,512]{2,1,0:T(8,128)(2,1)}, u32[]{:S(2)}, u32[]{:S(2)}) collective-permute-start(bf16[3,128,512]{2,1,0:T(8,128)(2,1)S(1)} %collective-permute-done.3.refs_4_), channel_id=1, source_target_pairs={{0,16},{16,32},{32,48},{48,0},{64,112},{80,64},{96,80},{112,96},{1... | collective-permute-start | bytes 1179656 | tf_op jit(solution)/shard_map/ppermute | solution.py:35
  31.9 0.0 collective-permute-done.10.refs_12_
  31.9 0.0 collective-permute-start.12
  31.9 0.0 collective-permute-done.2.refs_3_
  31.9 2.6 %collective-permute-start.6 = (bf16[3,128,512]{2,1,0:T(8,128)(2,1)S(1)}, bf16[3,128,512]{2,1,0:T(8,128)(2,1)}, u32[]{:S(2)}, u32[]{:S(2)}) collective-permute-start(bf16[3,128,512]{2,1,0:T(8,128)(2,1)S(1)} %collective-permute-done.2.refs_3_), channel_id=1, source_target_pairs={{0,8},{8,0},{1,9},{9,1},{2,10},{10,2},{3,11},{11,3},{4,12},{12,4},... | collective-permute-start | bytes 1179656 | tf_op jit(solution)/shard_map/ppermute | solution.py:35
  34.5 0.0 collective-permute-done.11.refs_13_
  34.5 3.2 %collective-permute-start.13 = (bf16[3,128,512]{2,1,0:T(8,128)(2,1)S(1)}, bf16[3,128,512]{2,1,0:T(8,128)(2,1)}, u32[]{:S(2)}, u32[]{:S(2)}) collective-permute-start(bf16[3,128,512]{2,1,0:T(8,128)(2,1)S(1)} %collective-permute-done.11.refs_13_), channel_id=1, source_target_pairs={{0,1},{1,2},{2,3},{3,4},{4,5},{5,6},{6,7},{7,0},{64,71},{65,64},{6... | collective-permute-start | bytes 1179656 | tf_op jit(solution)/shard_map/ppermute | solution.py:35
  37.7 0.1 stack.83.order
  37.8 3.2 %collective-permute-done.5.refs_6_ = bf16[3,128,512]{2,1,0:T(8,128)(2,1)} collective-permute-done((bf16[3,128,512]{2,1,0:T(8,128)(2,1)S(1)}, bf16[3,128,512]{2,1,0:T(8,128)(2,1)}, u32[]{:S(2)}, u32[]{:S(2)}) %collective-permute-start.5) | collective-permute-done | bytes 393248 | tf_op jit(solution)/shard_map/ppermute | solution.py:35
  41.1 0.0 collective-permute-done.4.refs_5_
  41.1 0.0 collective-permute-done.12.refs_14_
  41.1 0.0 collective-permute-done.6.refs_7_
  41.1 5.3 %collective-permute-done.13.refs_15_ = bf16[3,128,512]{2,1,0:T(8,128)(2,1)} collective-permute-done((bf16[3,128,512]{2,1,0:T(8,128)(2,1)S(1)}, bf16[3,128,512]{2,1,0:T(8,128)(2,1)}, u32[]{:S(2)}, u32[]{:S(2)}) %collective-permute-start.13) | collective-permute-done | bytes 393248 | tf_op jit(solution)/shard_map/ppermute | solution.py:35
  46.3 0.0 copy-start
  46.3 1.0 %copy-done = bf16[128,3,512]{2,0,1:T(8,128)(2,1)S(1)} copy-done((bf16[128,3,512]{2,0,1:T(8,128)(2,1)S(1)}, bf16[128,3,512]{2,0,1:T(8,128)(2,1)}, u32[]{:S(2)}) %copy-start) | copy-done | bytes 393240
  47.3 4.7 %shard_map.17.refs_16_ = f32[2,1024,256]{2,1,0:T(8,128)S(1)} custom-call(s32[20]{0:T(128)S(1)} %stack.83.order, bf16[3,128,512]{2,1,0:T(8,128)(2,1)S(1)} %bitcast.28, bf16[3,128,512]{2,1,0:T(8,128)(2,1)S(1)} %collective-permute-done.refs_1_, bf16[3,128,512]{2,1,0:T(8,128)(2,1)S(1)} %collective-permute-done.1.refs_2_, ...), custom_call_target="tpu_custom_call" | custom-call | tf_op jit(solution)/shard_map/pallas_call | solution.py:109
  52.0 1.2 %collective-permute-start.14 = (f32[2,1024,256]{2,1,0:T(8,128)S(1)}, f32[2,1024,256]{2,1,0:T(8,128)S(1)}, u32[]{:S(2)}, u32[]{:S(2)}) collective-permute-start(f32[2,1024,256]{2,1,0:T(8,128)S(1)} %shard_map.17.refs_16_), channel_id=1, source_target_pairs={{0,64},{64,0},{1,65},{65,1},{2,66},{66,2},{3,67},{67,3},{4,68},{68... | collective-permute-start | bytes 6291464 | tf_op jit(solution)/shard_map/ppermute | solution.py:35
  53.2 4.7 %shard_map.18 = f32[2,1024,256]{2,1,0:T(8,128)S(1)} custom-call(s32[20]{0:T(128)S(1)} %stack.83.order, bf16[3,128,512]{2,1,0:T(8,128)(2,1)S(1)} %bitcast.30, bf16[3,128,512]{2,1,0:T(8,128)(2,1)S(1)} %collective-permute-done.refs_1_, bf16[3,128,512]{2,1,0:T(8,128)(2,1)S(1)} %collective-permute-done.1.refs_2_, ...), custom_call_target="tpu_custom_call" | custom-call | tf_op jit(solution)/shard_map/pallas_call | solution.py:109
  57.9 0.0 collective-permute-done.14
  57.9 0.3 add.139
  58.2 34.6 %all_to_all.5 = f32[16,128,256]{2,1,0:T(8,128)} all-to-all(f32[16,128,256]{2,1,0:T(8,128)S(1)} %bitcast.32), channel_id=1, replica_groups=mesh['xl'=2,'core'=2,'y'=4,'xh'=2,'z'=8] {'xl','y','xh'}, dimensions={0} | all-to-all | bytes 4194304 | tf_op jit(solution)/shard_map/all_to_all | solution.py:176
  92.8 2.4 %shard_map.19 = f32[1,128,2048]{2,1,0:T(8,128)} custom-call(f32[2,8,128,256]{3,2,1,0:T(8,128)} %bitcast.33), custom_call_target="tpu_custom_call" | custom-call | tf_op jit(solution)/shard_map/pallas_call | solution.py:133
Async XLA Ops:
  0.0 14.5 %collective-permute-start.7 = (bf16[3,128,512]{2,1,0:T(8,128)(2,1)}, bf16[3,128,512]{2,1,0:T(8,128)(2,1)S(1)}, u32[]{:S(2)}, u32[]{:S(2)}) collective-permute-start(bf16[3,128,512]{2,1,0:T(8,128)(2,1)} %bitcast.23), channel_id=1, source_target_pairs={{0,1},{1,2},{2,3},{3,4},{4,5},{5,6},{6,7},{7,0},{64,71},{65,64},{6... | collective-permute-start | bytes 1179656 | tf_op jit(solution)/shard_map/ppermute | solution.py:35
  6.4 15.4 %collective-permute-start.8 = (bf16[3,128,512]{2,1,0:T(8,128)(2,1)}, bf16[3,128,512]{2,1,0:T(8,128)(2,1)S(1)}, u32[]{:S(2)}, u32[]{:S(2)}) collective-permute-start(bf16[3,128,512]{2,1,0:T(8,128)(2,1)} %bitcast.24), channel_id=1, source_target_pairs={{0,7},{1,0},{2,1},{3,2},{4,3},{5,4},{6,5},{7,6},{64,65},{65,66},{6... | collective-permute-start | bytes 1179656 | tf_op jit(solution)/shard_map/ppermute | solution.py:35
  6.4 15.4 %collective-permute-start = (bf16[3,128,512]{2,1,0:T(8,128)(2,1)}, bf16[3,128,512]{2,1,0:T(8,128)(2,1)S(1)}, u32[]{:S(2)}, u32[]{:S(2)}) collective-permute-start(bf16[3,128,512]{2,1,0:T(8,128)(2,1)} %bitcast.25), channel_id=1, source_target_pairs={{0,16},{16,32},{32,48},{48,0},{64,112},{80,64},{96,80},{112,96},{1... | collective-permute-start | bytes 1179656 | tf_op jit(solution)/shard_map/ppermute | solution.py:35
  14.5 8.9 %collective-permute-start.9 = (bf16[3,128,512]{2,1,0:T(8,128)(2,1)S(1)}, bf16[3,128,512]{2,1,0:T(8,128)(2,1)S(1)}, u32[]{:S(2)}, u32[]{:S(2)}) collective-permute-start(bf16[3,128,512]{2,1,0:T(8,128)(2,1)S(1)} %collective-permute-done.7.refs_9_), channel_id=1, source_target_pairs={{0,1},{1,2},{2,3},{3,4},{4,5},{5,6},{6,7},{7,0},{64,71},{65,64},{6... | collective-permute-start | bytes 1179656 | tf_op jit(solution)/shard_map/ppermute | solution.py:35
  17.8 10.9 %collective-permute-start.3 = (bf16[3,128,512]{2,1,0:T(8,128)(2,1)}, bf16[3,128,512]{2,1,0:T(8,128)(2,1)S(1)}, u32[]{:S(2)}, u32[]{:S(2)}) collective-permute-start(bf16[3,128,512]{2,1,0:T(8,128)(2,1)} %bitcast.26), channel_id=1, source_target_pairs={{0,8},{8,0},{1,9},{9,1},{2,10},{10,2},{3,11},{11,3},{4,12},{12,4},... | collective-permute-start | bytes 1179656 | tf_op jit(solution)/shard_map/ppermute | solution.py:35
  20.6 9.4 %collective-permute-start.1 = (bf16[3,128,512]{2,1,0:T(8,128)(2,1)}, bf16[3,128,512]{2,1,0:T(8,128)(2,1)S(1)}, u32[]{:S(2)}, u32[]{:S(2)}) collective-permute-start(bf16[3,128,512]{2,1,0:T(8,128)(2,1)} %bitcast.27), channel_id=1, source_target_pairs={{0,48},{16,0},{32,16},{48,32},{64,80},{80,96},{96,112},{112,64},{1... | collective-permute-start | bytes 1179656 | tf_op jit(solution)/shard_map/ppermute | solution.py:35
  21.9 10.1 %collective-permute-start.10 = (bf16[3,128,512]{2,1,0:T(8,128)(2,1)S(1)}, bf16[3,128,512]{2,1,0:T(8,128)(2,1)S(1)}, u32[]{:S(2)}, u32[]{:S(2)}) collective-permute-start(bf16[3,128,512]{2,1,0:T(8,128)(2,1)S(1)} %collective-permute-done.8.refs_10_), channel_id=1, source_target_pairs={{0,7},{1,0},{2,1},{3,2},{4,3},{5,4},{6,5},{7,6},{64,65},{65,66},{6... | collective-permute-start | bytes 1179656 | tf_op jit(solution)/shard_map/ppermute | solution.py:35
  21.9 10.1 %collective-permute-start.2 = (bf16[3,128,512]{2,1,0:T(8,128)(2,1)S(1)}, bf16[3,128,512]{2,1,0:T(8,128)(2,1)S(1)}, u32[]{:S(2)}, u32[]{:S(2)}) collective-permute-start(bf16[3,128,512]{2,1,0:T(8,128)(2,1)S(1)} %collective-permute-done.refs_1_), channel_id=1, source_target_pairs={{0,16},{16,32},{32,48},{48,0},{64,112},{80,64},{96,80},{112,96},{1... | collective-permute-start | bytes 1179656 | tf_op jit(solution)/shard_map/ppermute | solution.py:35
  23.4 11.1 %collective-permute-start.11 = (bf16[3,128,512]{2,1,0:T(8,128)(2,1)S(1)}, bf16[3,128,512]{2,1,0:T(8,128)(2,1)S(1)}, u32[]{:S(2)}, u32[]{:S(2)}) collective-permute-start(bf16[3,128,512]{2,1,0:T(8,128)(2,1)S(1)} %collective-permute-done.9.refs_11_), channel_id=1, source_target_pairs={{0,1},{1,2},{2,3},{3,4},{4,5},{5,6},{6,7},{7,0},{64,71},{65,64},{6... | collective-permute-start | bytes 1179656 | tf_op jit(solution)/shard_map/ppermute | solution.py:35
  28.7 12.4 %collective-permute-start.5 = (bf16[3,128,512]{2,1,0:T(8,128)(2,1)S(1)}, bf16[3,128,512]{2,1,0:T(8,128)(2,1)}, u32[]{:S(2)}, u32[]{:S(2)}) collective-permute-start(bf16[3,128,512]{2,1,0:T(8,128)(2,1)S(1)} %collective-permute-done.3.refs_4_), channel_id=1, source_target_pairs={{0,48},{16,0},{32,16},{48,32},{64,80},{80,96},{96,112},{112,64},{1... | collective-permute-start | bytes 1179656 | tf_op jit(solution)/shard_map/ppermute | solution.py:35
  30.0 11.1 %collective-permute-start.4 = (bf16[3,128,512]{2,1,0:T(8,128)(2,1)S(1)}, bf16[3,128,512]{2,1,0:T(8,128)(2,1)}, u32[]{:S(2)}, u32[]{:S(2)}) collective-permute-start(bf16[3,128,512]{2,1,0:T(8,128)(2,1)S(1)} %collective-permute-done.3.refs_4_), channel_id=1, source_target_pairs={{0,16},{16,32},{32,48},{48,0},{64,112},{80,64},{96,80},{112,96},{1... | collective-permute-start | bytes 1179656 | tf_op jit(solution)/shard_map/ppermute | solution.py:35
  31.9 9.1 %collective-permute-start.12 = (bf16[3,128,512]{2,1,0:T(8,128)(2,1)S(1)}, bf16[3,128,512]{2,1,0:T(8,128)(2,1)}, u32[]{:S(2)}, u32[]{:S(2)}) collective-permute-start(bf16[3,128,512]{2,1,0:T(8,128)(2,1)S(1)} %collective-permute-done.10.refs_12_), channel_id=1, source_target_pairs={{0,7},{1,0},{2,1},{3,2},{4,3},{5,4},{6,5},{7,6},{64,65},{65,66},{6... | collective-permute-start | bytes 1179656 | tf_op jit(solution)/shard_map/ppermute | solution.py:35
  31.9 9.1 %collective-permute-start.6 = (bf16[3,128,512]{2,1,0:T(8,128)(2,1)S(1)}, bf16[3,128,512]{2,1,0:T(8,128)(2,1)}, u32[]{:S(2)}, u32[]{:S(2)}) collective-permute-start(bf16[3,128,512]{2,1,0:T(8,128)(2,1)S(1)} %collective-permute-done.2.refs_3_), channel_id=1, source_target_pairs={{0,8},{8,0},{1,9},{9,1},{2,10},{10,2},{3,11},{11,3},{4,12},{12,4},... | collective-permute-start | bytes 1179656 | tf_op jit(solution)/shard_map/ppermute | solution.py:35
  34.5 11.9 %collective-permute-start.13 = (bf16[3,128,512]{2,1,0:T(8,128)(2,1)S(1)}, bf16[3,128,512]{2,1,0:T(8,128)(2,1)}, u32[]{:S(2)}, u32[]{:S(2)}) collective-permute-start(bf16[3,128,512]{2,1,0:T(8,128)(2,1)S(1)} %collective-permute-done.11.refs_13_), channel_id=1, source_target_pairs={{0,1},{1,2},{2,3},{3,4},{4,5},{5,6},{6,7},{7,0},{64,71},{65,64},{6... | collective-permute-start | bytes 1179656 | tf_op jit(solution)/shard_map/ppermute | solution.py:35
  46.3 1.0 %copy-start = (bf16[128,3,512]{2,0,1:T(8,128)(2,1)S(1)}, bf16[128,3,512]{2,0,1:T(8,128)(2,1)}, u32[]{:S(2)}) copy-start(bf16[128,3,512]{2,0,1:T(8,128)(2,1)} %param.1) | copy-start | bytes 1179652
  52.0 5.9 %collective-permute-start.14 = (f32[2,1024,256]{2,1,0:T(8,128)S(1)}, f32[2,1024,256]{2,1,0:T(8,128)S(1)}, u32[]{:S(2)}, u32[]{:S(2)}) collective-permute-start(f32[2,1024,256]{2,1,0:T(8,128)S(1)} %shard_map.17.refs_16_), channel_id=1, source_target_pairs={{0,64},{64,0},{1,65},{65,1},{2,66},{66,2},{3,67},{67,3},{4,68},{68... | collective-permute-start | bytes 6291464 | tf_op jit(solution)/shard_map/ppermute | solution.py:35

commit v6 on v5

--- a/solution.py
+++ b/solution.py
@@ -82,20 +82,20 @@
     for n in range(half_slots):
         for c in column_copies[n]:
             c.wait()
-        for t in range(0, 8, 2):
+        for t in range(0, 8, 4):
             if n == 0:
-                for k in range(t, t + 2):
+                for k in range(t, t + 4):
                     row_copies[k].wait()
             total = None
             for a in range(aux):
                 part = lax.dot_general(
-                    rows[a, t * height : (t + 2) * height],
+                    rows[a, t * height : (t + 4) * height],
                     columns[a, n * 16 * sub : (n + 1) * 16 * sub],
                     (((1,), (1,)), ((), ())),
                     preferred_element_type=jnp.float32,
                 )
                 total = part if total is None else total + part
-            for k in range(t, t + 2):
+            for k in range(t, t + 4):
                 place = pl.multiple_of(order[k] * height, height)
                 for side in range(2):
                     targets[n][side, pl.ds(place, height), :] = total[

time: 95.4 us -> 94.5 us (level)
  no operation moved by 1% of the time
where the time goes in v6:
time: 94.5 us; the launch traced here: 94.2 us
  blocking collectives  34.6 us (37%)
  starting transfers between devices  30.6 us (32%)
  waiting for transfers between devices  16.6 us (18%)
  Pallas kernels  11 us (12%)
  local copies, waits for them, and re-layouts  1.09 us (1%)
    all_to_all x1, blocking collectives, per_device(): lax.all_to_all(parts, ('xl', 'y', 'xh'), split_axis=0, concat_axis=0, til...  34.6 us
    ppermute x15, starting transfers between devices, move(): return lax.ppermute(value, axes, pairs)  30.6 us
    ppermute x15, waiting for transfers between devices, move(): return lax.ppermute(value, axes, pairs)  16.6 us
    pallas_call x2, Pallas kernels, products(): pl.pallas_call(functools.partial(product_kernel, slots), out_shape=[shape...  8.59 us
    pallas_call x1, Pallas kernels, assemble(): pl.pallas_call(assemble_kernel, grid=(count // step,), out_shape=jax.Shap...  2.39 us
  transfers between devices with their start and end apart: 15, of which 4 were waited for; matrix products, arithmetic and copies ran while one was open for 0% of the time, Pallas kernels for 5%

profile of v6, /device:TPU:1, one launch (start us, length us, event | category | flops | bytes accessed | tf_op | source)
XLA Modules:
  0.0 94.2 jit_solution(3749166229825899727)
XLA Ops:
  0.0 6.4 %collective-permute-start.7 = (bf16[3,128,512]{2,1,0:T(8,128)(2,1)}, bf16[3,128,512]{2,1,0:T(8,128)(2,1)S(1)}, u32[]{:S(2)}, u32[]{:S(2)}) collective-permute-start(bf16[3,128,512]{2,1,0:T(8,128)(2,1)} %bitcast.23), channel_id=1, source_target_pairs={{0,1},{1,2},{2,3},{3,4},{4,5},{5,6},{6,7},{7,0},{64,71},{65,64},{6... | collective-permute-start | bytes 1179656 | tf_op jit(solution)/shard_map/ppermute | solution.py:35
  6.4 0.0 collective-permute-start.8
  6.4 2.7 %collective-permute-start = (bf16[3,128,512]{2,1,0:T(8,128)(2,1)}, bf16[3,128,512]{2,1,0:T(8,128)(2,1)S(1)}, u32[]{:S(2)}, u32[]{:S(2)}) collective-permute-start(bf16[3,128,512]{2,1,0:T(8,128)(2,1)} %bitcast.25), channel_id=1, source_target_pairs={{0,16},{16,32},{32,48},{48,0},{64,112},{80,64},{96,80},{112,96},{1... | collective-permute-start | bytes 1179656 | tf_op jit(solution)/shard_map/ppermute | solution.py:35
  9.1 5.4 %collective-permute-done.7.refs_9_ = bf16[3,128,512]{2,1,0:T(8,128)(2,1)S(1)} collective-permute-done((bf16[3,128,512]{2,1,0:T(8,128)(2,1)}, bf16[3,128,512]{2,1,0:T(8,128)(2,1)S(1)}, u32[]{:S(2)}, u32[]{:S(2)}) %collective-permute-start.7) | collective-permute-done | bytes 393248 | tf_op jit(solution)/shard_map/ppermute | solution.py:35
  14.5 3.3 %collective-permute-start.9 = (bf16[3,128,512]{2,1,0:T(8,128)(2,1)S(1)}, bf16[3,128,512]{2,1,0:T(8,128)(2,1)S(1)}, u32[]{:S(2)}, u32[]{:S(2)}) collective-permute-start(bf16[3,128,512]{2,1,0:T(8,128)(2,1)S(1)} %collective-permute-done.7.refs_9_), channel_id=1, source_target_pairs={{0,1},{1,2},{2,3},{3,4},{4,5},{5,6},{6,7},{7,0},{64,71},{65,64},{6... | collective-permute-start | bytes 1179656 | tf_op jit(solution)/shard_map/ppermute | solution.py:35
  17.8 2.7 %collective-permute-start.3 = (bf16[3,128,512]{2,1,0:T(8,128)(2,1)}, bf16[3,128,512]{2,1,0:T(8,128)(2,1)S(1)}, u32[]{:S(2)}, u32[]{:S(2)}) collective-permute-start(bf16[3,128,512]{2,1,0:T(8,128)(2,1)} %bitcast.26), channel_id=1, source_target_pairs={{0,8},{8,0},{1,9},{9,1},{2,10},{10,2},{3,11},{11,3},{4,12},{12,4},... | collective-permute-start | bytes 1179656 | tf_op jit(solution)/shard_map/ppermute | solution.py:35
  20.6 1.3 %collective-permute-start.1 = (bf16[3,128,512]{2,1,0:T(8,128)(2,1)}, bf16[3,128,512]{2,1,0:T(8,128)(2,1)S(1)}, u32[]{:S(2)}, u32[]{:S(2)}) collective-permute-start(bf16[3,128,512]{2,1,0:T(8,128)(2,1)} %bitcast.27), channel_id=1, source_target_pairs={{0,48},{16,0},{32,16},{48,32},{64,80},{80,96},{96,112},{112,64},{1... | collective-permute-start | bytes 1179656 | tf_op jit(solution)/shard_map/ppermute | solution.py:35
  21.8 0.0 collective-permute-done.8.refs_10_
  21.9 0.0 collective-permute-start.10
  21.9 0.0 collective-permute-done.refs_1_
  21.9 1.5 %collective-permute-start.2 = (bf16[3,128,512]{2,1,0:T(8,128)(2,1)S(1)}, bf16[3,128,512]{2,1,0:T(8,128)(2,1)S(1)}, u32[]{:S(2)}, u32[]{:S(2)}) collective-permute-start(bf16[3,128,512]{2,1,0:T(8,128)(2,1)S(1)} %collective-permute-done.refs_1_), channel_id=1, source_target_pairs={{0,16},{16,32},{32,48},{48,0},{64,112},{80,64},{96,80},{112,96},{1... | collective-permute-start | bytes 1179656 | tf_op jit(solution)/shard_map/ppermute | solution.py:35
  23.4 0.0 collective-permute-done.9.refs_11_
  23.4 2.6 %collective-permute-start.11 = (bf16[3,128,512]{2,1,0:T(8,128)(2,1)S(1)}, bf16[3,128,512]{2,1,0:T(8,128)(2,1)S(1)}, u32[]{:S(2)}, u32[]{:S(2)}) collective-permute-start(bf16[3,128,512]{2,1,0:T(8,128)(2,1)S(1)} %collective-permute-done.9.refs_11_), channel_id=1, source_target_pairs={{0,1},{1,2},{2,3},{3,4},{4,5},{5,6},{6,7},{7,0},{64,71},{65,64},{6... | collective-permute-start | bytes 1179656 | tf_op jit(solution)/shard_map/ppermute | solution.py:35
  26.0 2.7 %collective-permute-done.3.refs_4_ = bf16[3,128,512]{2,1,0:T(8,128)(2,1)S(1)} collective-permute-done((bf16[3,128,512]{2,1,0:T(8,128)(2,1)}, bf16[3,128,512]{2,1,0:T(8,128)(2,1)S(1)}, u32[]{:S(2)}, u32[]{:S(2)}) %collective-permute-start.3) | collective-permute-done | bytes 393248 | tf_op jit(solution)/shard_map/ppermute | solution.py:35
  28.7 1.3 %collective-permute-start.5 = (bf16[3,128,512]{2,1,0:T(8,128)(2,1)S(1)}, bf16[3,128,512]{2,1,0:T(8,128)(2,1)}, u32[]{:S(2)}, u32[]{:S(2)}) collective-permute-start(bf16[3,128,512]{2,1,0:T(8,128)(2,1)S(1)} %collective-permute-done.3.refs_4_), channel_id=1, source_target_pairs={{0,48},{16,0},{32,16},{48,32},{64,80},{80,96},{96,112},{112,64},{1... | collective-permute-start | bytes 1179656 | tf_op jit(solution)/shard_map/ppermute | solution.py:35
  30.0 0.0 collective-permute-done.1.refs_2_
  30.0 2.0 %collective-permute-start.4 = (bf16[3,128,512]{2,1,0:T(8,128)(2,1)S(1)}, bf16[3,128,512]{2,1,0:T(8,128)(2,1)}, u32[]{:S(2)}, u32[]{:S(2)}) collective-permute-start(bf16[3,128,512]{2,1,0:T(8,128)(2,1)S(1)} %collective-permute-done.3.refs_4_), channel_id=1, source_target_pairs={{0,16},{16,32},{32,48},{48,0},{64,112},{80,64},{96,80},{112,96},{1... | collective-permute-start | bytes 1179656 | tf_op jit(solution)/shard_map/ppermute | solution.py:35
  31.9 0.0 collective-permute-done.10.refs_12_
  31.9 0.0 collective-permute-start.12
  31.9 0.0 collective-permute-done.2.refs_3_
  31.9 2.6 %collective-permute-start.6 = (bf16[3,128,512]{2,1,0:T(8,128)(2,1)S(1)}, bf16[3,128,512]{2,1,0:T(8,128)(2,1)}, u32[]{:S(2)}, u32[]{:S(2)}) collective-permute-start(bf16[3,128,512]{2,1,0:T(8,128)(2,1)S(1)} %collective-permute-done.2.refs_3_), channel_id=1, source_target_pairs={{0,8},{8,0},{1,9},{9,1},{2,10},{10,2},{3,11},{11,3},{4,12},{12,4},... | collective-permute-start | bytes 1179656 | tf_op jit(solution)/shard_map/ppermute | solution.py:35
  34.5 0.0 collective-permute-done.11.refs_13_
  34.5 3.2 %collective-permute-start.13 = (bf16[3,128,512]{2,1,0:T(8,128)(2,1)S(1)}, bf16[3,128,512]{2,1,0:T(8,128)(2,1)}, u32[]{:S(2)}, u32[]{:S(2)}) collective-permute-start(bf16[3,128,512]{2,1,0:T(8,128)(2,1)S(1)} %collective-permute-done.11.refs_13_), channel_id=1, source_target_pairs={{0,1},{1,2},{2,3},{3,4},{4,5},{5,6},{6,7},{7,0},{64,71},{65,64},{6... | collective-permute-start | bytes 1179656 | tf_op jit(solution)/shard_map/ppermute | solution.py:35
  37.7 0.1 stack.83.order
  37.8 3.2 %collective-permute-done.5.refs_6_ = bf16[3,128,512]{2,1,0:T(8,128)(2,1)} collective-permute-done((bf16[3,128,512]{2,1,0:T(8,128)(2,1)S(1)}, bf16[3,128,512]{2,1,0:T(8,128)(2,1)}, u32[]{:S(2)}, u32[]{:S(2)}) %collective-permute-start.5) | collective-permute-done | bytes 393248 | tf_op jit(solution)/shard_map/ppermute | solution.py:35
  41.1 0.0 collective-permute-done.4.refs_5_
  41.1 0.0 collective-permute-done.12.refs_14_
  41.1 0.0 collective-permute-done.6.refs_7_
  41.1 5.3 %collective-permute-done.13.refs_15_ = bf16[3,128,512]{2,1,0:T(8,128)(2,1)} collective-permute-done((bf16[3,128,512]{2,1,0:T(8,128)(2,1)S(1)}, bf16[3,128,512]{2,1,0:T(8,128)(2,1)}, u32[]{:S(2)}, u32[]{:S(2)}) %collective-permute-start.13) | collective-permute-done | bytes 393248 | tf_op jit(solution)/shard_map/ppermute | solution.py:35
  46.3 0.0 copy-start
  46.3 1.0 %copy-done = bf16[128,3,512]{2,0,1:T(8,128)(2,1)S(1)} copy-done((bf16[128,3,512]{2,0,1:T(8,128)(2,1)S(1)}, bf16[128,3,512]{2,0,1:T(8,128)(2,1)}, u32[]{:S(2)}) %copy-start) | copy-done | bytes 393240
  47.3 4.3 %shard_map.17.refs_16_ = f32[2,1024,256]{2,1,0:T(8,128)S(1)} custom-call(s32[20]{0:T(128)S(1)} %stack.83.order, bf16[3,128,512]{2,1,0:T(8,128)(2,1)S(1)} %bitcast.28, bf16[3,128,512]{2,1,0:T(8,128)(2,1)S(1)} %collective-permute-done.refs_1_, bf16[3,128,512]{2,1,0:T(8,128)(2,1)S(1)} %collective-permute-done.1.refs_2_, ...), custom_call_target="tpu_custom_call" | custom-call | tf_op jit(solution)/shard_map/pallas_call | solution.py:109
  51.6 1.0 %collective-permute-start.14 = (f32[2,1024,256]{2,1,0:T(8,128)S(1)}, f32[2,1024,256]{2,1,0:T(8,128)S(1)}, u32[]{:S(2)}, u32[]{:S(2)}) collective-permute-start(f32[2,1024,256]{2,1,0:T(8,128)S(1)} %shard_map.17.refs_16_), channel_id=1, source_target_pairs={{0,64},{64,0},{1,65},{65,1},{2,66},{66,2},{3,67},{67,3},{4,68},{68... | collective-permute-start | bytes 6291464 | tf_op jit(solution)/shard_map/ppermute | solution.py:35
  52.6 4.3 %shard_map.18 = f32[2,1024,256]{2,1,0:T(8,128)S(1)} custom-call(s32[20]{0:T(128)S(1)} %stack.83.order, bf16[3,128,512]{2,1,0:T(8,128)(2,1)S(1)} %bitcast.30, bf16[3,128,512]{2,1,0:T(8,128)(2,1)S(1)} %collective-permute-done.refs_1_, bf16[3,128,512]{2,1,0:T(8,128)(2,1)S(1)} %collective-permute-done.1.refs_2_, ...), custom_call_target="tpu_custom_call" | custom-call | tf_op jit(solution)/shard_map/pallas_call | solution.py:109
  57.0 0.0 collective-permute-done.14
  57.0 0.3 add.139
  57.2 34.6 %all_to_all.5 = f32[16,128,256]{2,1,0:T(8,128)} all-to-all(f32[16,128,256]{2,1,0:T(8,128)S(1)} %bitcast.32), channel_id=1, replica_groups=mesh['xl'=2,'core'=2,'y'=4,'xh'=2,'z'=8] {'xl','y','xh'}, dimensions={0} | all-to-all | bytes 4194304 | tf_op jit(solution)/shard_map/all_to_all | solution.py:176
  91.8 2.4 %shard_map.19 = f32[1,128,2048]{2,1,0:T(8,128)} custom-call(f32[2,8,128,256]{3,2,1,0:T(8,128)} %bitcast.33), custom_call_target="tpu_custom_call" | custom-call | tf_op jit(solution)/shard_map/pallas_call | solution.py:133
Async XLA Ops:
  0.0 14.5 %collective-permute-start.7 = (bf16[3,128,512]{2,1,0:T(8,128)(2,1)}, bf16[3,128,512]{2,1,0:T(8,128)(2,1)S(1)}, u32[]{:S(2)}, u32[]{:S(2)}) collective-permute-start(bf16[3,128,512]{2,1,0:T(8,128)(2,1)} %bitcast.23), channel_id=1, source_target_pairs={{0,1},{1,2},{2,3},{3,4},{4,5},{5,6},{6,7},{7,0},{64,71},{65,64},{6... | collective-permute-start | bytes 1179656 | tf_op jit(solution)/shard_map/ppermute | solution.py:35
  6.4 15.4 %collective-permute-start.8 = (bf16[3,128,512]{2,1,0:T(8,128)(2,1)}, bf16[3,128,512]{2,1,0:T(8,128)(2,1)S(1)}, u32[]{:S(2)}, u32[]{:S(2)}) collective-permute-start(bf16[3,128,512]{2,1,0:T(8,128)(2,1)} %bitcast.24), channel_id=1, source_target_pairs={{0,7},{1,0},{2,1},{3,2},{4,3},{5,4},{6,5},{7,6},{64,65},{65,66},{6... | collective-permute-start | bytes 1179656 | tf_op jit(solution)/shard_map/ppermute | solution.py:35
  6.4 15.4 %collective-permute-start = (bf16[3,128,512]{2,1,0:T(8,128)(2,1)}, bf16[3,128,512]{2,1,0:T(8,128)(2,1)S(1)}, u32[]{:S(2)}, u32[]{:S(2)}) collective-permute-start(bf16[3,128,512]{2,1,0:T(8,128)(2,1)} %bitcast.25), channel_id=1, source_target_pairs={{0,16},{16,32},{32,48},{48,0},{64,112},{80,64},{96,80},{112,96},{1... | collective-permute-start | bytes 1179656 | tf_op jit(solution)/shard_map/ppermute | solution.py:35
  14.5 8.9 %collective-permute-start.9 = (bf16[3,128,512]{2,1,0:T(8,128)(2,1)S(1)}, bf16[3,128,512]{2,1,0:T(8,128)(2,1)S(1)}, u32[]{:S(2)}, u32[]{:S(2)}) collective-permute-start(bf16[3,128,512]{2,1,0:T(8,128)(2,1)S(1)} %collective-permute-done.7.refs_9_), channel_id=1, source_target_pairs={{0,1},{1,2},{2,3},{3,4},{4,5},{5,6},{6,7},{7,0},{64,71},{65,64},{6... | collective-permute-start | bytes 1179656 | tf_op jit(solution)/shard_map/ppermute | solution.py:35
  17.8 10.9 %collective-permute-start.3 = (bf16[3,128,512]{2,1,0:T(8,128)(2,1)}, bf16[3,128,512]{2,1,0:T(8,128)(2,1)S(1)}, u32[]{:S(2)}, u32[]{:S(2)}) collective-permute-start(bf16[3,128,512]{2,1,0:T(8,128)(2,1)} %bitcast.26), channel_id=1, source_target_pairs={{0,8},{8,0},{1,9},{9,1},{2,10},{10,2},{3,11},{11,3},{4,12},{12,4},... | collective-permute-start | bytes 1179656 | tf_op jit(solution)/shard_map/ppermute | solution.py:35
  20.6 9.4 %collective-permute-start.1 = (bf16[3,128,512]{2,1,0:T(8,128)(2,1)}, bf16[3,128,512]{2,1,0:T(8,128)(2,1)S(1)}, u32[]{:S(2)}, u32[]{:S(2)}) collective-permute-start(bf16[3,128,512]{2,1,0:T(8,128)(2,1)} %bitcast.27), channel_id=1, source_target_pairs={{0,48},{16,0},{32,16},{48,32},{64,80},{80,96},{96,112},{112,64},{1... | collective-permute-start | bytes 1179656 | tf_op jit(solution)/shard_map/ppermute | solution.py:35
  21.9 10.1 %collective-permute-start.10 = (bf16[3,128,512]{2,1,0:T(8,128)(2,1)S(1)}, bf16[3,128,512]{2,1,0:T(8,128)(2,1)S(1)}, u32[]{:S(2)}, u32[]{:S(2)}) collective-permute-start(bf16[3,128,512]{2,1,0:T(8,128)(2,1)S(1)} %collective-permute-done.8.refs_10_), channel_id=1, source_target_pairs={{0,7},{1,0},{2,1},{3,2},{4,3},{5,4},{6,5},{7,6},{64,65},{65,66},{6... | collective-permute-start | bytes 1179656 | tf_op jit(solution)/shard_map/ppermute | solution.py:35
  21.9 10.1 %collective-permute-start.2 = (bf16[3,128,512]{2,1,0:T(8,128)(2,1)S(1)}, bf16[3,128,512]{2,1,0:T(8,128)(2,1)S(1)}, u32[]{:S(2)}, u32[]{:S(2)}) collective-permute-start(bf16[3,128,512]{2,1,0:T(8,128)(2,1)S(1)} %collective-permute-done.refs_1_), channel_id=1, source_target_pairs={{0,16},{16,32},{32,48},{48,0},{64,112},{80,64},{96,80},{112,96},{1... | collective-permute-start | bytes 1179656 | tf_op jit(solution)/shard_map/ppermute | solution.py:35
  23.4 11.1 %collective-permute-start.11 = (bf16[3,128,512]{2,1,0:T(8,128)(2,1)S(1)}, bf16[3,128,512]{2,1,0:T(8,128)(2,1)S(1)}, u32[]{:S(2)}, u32[]{:S(2)}) collective-permute-start(bf16[3,128,512]{2,1,0:T(8,128)(2,1)S(1)} %collective-permute-done.9.refs_11_), channel_id=1, source_target_pairs={{0,1},{1,2},{2,3},{3,4},{4,5},{5,6},{6,7},{7,0},{64,71},{65,64},{6... | collective-permute-start | bytes 1179656 | tf_op jit(solution)/shard_map/ppermute | solution.py:35
  28.7 12.4 %collective-permute-start.5 = (bf16[3,128,512]{2,1,0:T(8,128)(2,1)S(1)}, bf16[3,128,512]{2,1,0:T(8,128)(2,1)}, u32[]{:S(2)}, u32[]{:S(2)}) collective-permute-start(bf16[3,128,512]{2,1,0:T(8,128)(2,1)S(1)} %collective-permute-done.3.refs_4_), channel_id=1, source_target_pairs={{0,48},{16,0},{32,16},{48,32},{64,80},{80,96},{96,112},{112,64},{1... | collective-permute-start | bytes 1179656 | tf_op jit(solution)/shard_map/ppermute | solution.py:35
  30.0 11.1 %collective-permute-start.4 = (bf16[3,128,512]{2,1,0:T(8,128)(2,1)S(1)}, bf16[3,128,512]{2,1,0:T(8,128)(2,1)}, u32[]{:S(2)}, u32[]{:S(2)}) collective-permute-start(bf16[3,128,512]{2,1,0:T(8,128)(2,1)S(1)} %collective-permute-done.3.refs_4_), channel_id=1, source_target_pairs={{0,16},{16,32},{32,48},{48,0},{64,112},{80,64},{96,80},{112,96},{1... | collective-permute-start | bytes 1179656 | tf_op jit(solution)/shard_map/ppermute | solution.py:35
  31.9 9.1 %collective-permute-start.12 = (bf16[3,128,512]{2,1,0:T(8,128)(2,1)S(1)}, bf16[3,128,512]{2,1,0:T(8,128)(2,1)}, u32[]{:S(2)}, u32[]{:S(2)}) collective-permute-start(bf16[3,128,512]{2,1,0:T(8,128)(2,1)S(1)} %collective-permute-done.10.refs_12_), channel_id=1, source_target_pairs={{0,7},{1,0},{2,1},{3,2},{4,3},{5,4},{6,5},{7,6},{64,65},{65,66},{6... | collective-permute-start | bytes 1179656 | tf_op jit(solution)/shard_map/ppermute | solution.py:35
  31.9 9.1 %collective-permute-start.6 = (bf16[3,128,512]{2,1,0:T(8,128)(2,1)S(1)}, bf16[3,128,512]{2,1,0:T(8,128)(2,1)}, u32[]{:S(2)}, u32[]{:S(2)}) collective-permute-start(bf16[3,128,512]{2,1,0:T(8,128)(2,1)S(1)} %collective-permute-done.2.refs_3_), channel_id=1, source_target_pairs={{0,8},{8,0},{1,9},{9,1},{2,10},{10,2},{3,11},{11,3},{4,12},{12,4},... | collective-permute-start | bytes 1179656 | tf_op jit(solution)/shard_map/ppermute | solution.py:35
  34.5 11.9 %collective-permute-start.13 = (bf16[3,128,512]{2,1,0:T(8,128)(2,1)S(1)}, bf16[3,128,512]{2,1,0:T(8,128)(2,1)}, u32[]{:S(2)}, u32[]{:S(2)}) collective-permute-start(bf16[3,128,512]{2,1,0:T(8,128)(2,1)S(1)} %collective-permute-done.11.refs_13_), channel_id=1, source_target_pairs={{0,1},{1,2},{2,3},{3,4},{4,5},{5,6},{6,7},{7,0},{64,71},{65,64},{6... | collective-permute-start | bytes 1179656 | tf_op jit(solution)/shard_map/ppermute | solution.py:35
  46.3 1.0 %copy-start = (bf16[128,3,512]{2,0,1:T(8,128)(2,1)S(1)}, bf16[128,3,512]{2,0,1:T(8,128)(2,1)}, u32[]{:S(2)}) copy-start(bf16[128,3,512]{2,0,1:T(8,128)(2,1)} %param.1) | copy-start | bytes 1179652
  51.6 5.3 %collective-permute-start.14 = (f32[2,1024,256]{2,1,0:T(8,128)S(1)}, f32[2,1024,256]{2,1,0:T(8,128)S(1)}, u32[]{:S(2)}, u32[]{:S(2)}) collective-permute-start(f32[2,1024,256]{2,1,0:T(8,128)S(1)} %shard_map.17.refs_16_), channel_id=1, source_target_pairs={{0,64},{64,0},{1,65},{65,1},{2,66},{66,2},{3,67},{67,3},{4,68},{68... | collective-permute-start | bytes 6291464 | tf_op jit(solution)/shard_map/ppermute | solution.py:35
